TPU v7x, 256 devices: a whole 4x4x8 slice. The times are simulated.
256 devices in a mesh: tile: 32 (over x_lo, z, core), corner: 8 (over y, x_hi).
Axes of the slice: x: 4 (x_hi: 2, x_lo: 2; x = x_hi * 2 + x_lo), y: 4, z: 8, core: 2. Of those that a mesh axis runs over, the one named last changes fastest.
Arguments:
- mask_logits: float32 [4096, 1024], P('tile'), may hold values from -4 to 4
- target: int32 [4096, 1024], P('tile'), may hold values 0 or 1
- kernels: float32 [4, 12, 25, 384], replicated, may hold values from -0.9 to 0.9
- dose_levels: float32 [4], replicated, may hold values from 0.8 to 1.2
Outputs:
- pv_band: float32 [4096, 1024], P('tile', 'corner')
- logit_grad: float32 [4096, 1024], P('tile', 'corner')
All inputs are finite; a program needn't handle non-finite values. No bound on the sum of `target` on one device may be relied on, other than what follows from the above.
Results may differ from a plain program's by a relative error of at most 0.024.
Values may be sent and summed in bfloat16 or wider, within the bound.
No kernel may reach another device: no remote copies, remote signals or barrier semaphores. Data moves between devices by JAX's collectives and lax.ppermute only.
A program may use at most 128 MiB of HBM per device.

v0:
```python
import math

import jax
import jax.numpy as jnp
from jax import lax
from jax.sharding import PartitionSpec as P

STEEPNESS = 4.0
THRESHOLD = 1.0
SHARPNESS = 12.0


def extended_2(value, sides, width):
    for axis, dim in sides:
        size, length = (lax.axis_size(axis), value.shape[dim])
        up = [(i, (i + 1) % size) for i in range(size - 1)]
        down = [(j, i) for i, j in up]
        last = lax.slice_in_dim(value, length - width, length, axis=dim)
        initial = lax.slice_in_dim(value, 0, width, axis=dim)
        before = lax.ppermute(last, axis, up)
        after = lax.ppermute(initial, axis, down)
        value = jnp.concatenate([before, value, after], axis=dim)
    return value


def passed_along(value, axis, by):
    size = lax.axis_size(axis)
    pairs = [(i, i + by) for i in range(size) if 0 <= i + by < size]
    return lax.ppermute(value, axis, pairs)


def dft_tables(columns, half_freq):
    column_ids = jnp.arange(columns, dtype=jnp.int32)
    frequencies = jnp.arange(half_freq, dtype=jnp.int32) - half_freq // 2
    phases = frequencies[:, None] * column_ids[None, :] % columns
    angles = 2.0 * math.pi / columns * phases.astype(jnp.float32)
    factor = 1.0 / math.sqrt(columns)
    cosine = jnp.cos(angles) * factor
    sine_table = jnp.sin(angles) * factor
    forward = jnp.concatenate([cosine.T, -sine_table.T], axis=1)
    inverse = jnp.concatenate(
        [
            jnp.concatenate([cosine, sine_table], axis=1),
            jnp.concatenate([-sine_table, cosine], axis=1),
        ],
        axis=0,
    )
    return (forward, inverse)


def mix_rows(extended, kernel):
    kernel_taps = kernel.shape[0]
    half_freq = kernel.shape[1] // 2
    row_count = extended.shape[0] - kernel_taps + 1
    field_re = None
    field_im = None
    for offset in range(kernel_taps):
        ext_re = extended[offset : offset + row_count, :half_freq]
        ext_im = extended[offset : offset + row_count, half_freq:]
        kern_re = kernel[offset, :half_freq]
        kern_im = kernel[offset, half_freq:]
        part_re = ext_re * kern_re - ext_im * kern_im
        part_im = ext_re * kern_im + ext_im * kern_re
        field_re = part_re if field_re is None else field_re + part_re
        field_im = part_im if field_im is None else field_im + part_im
    return jnp.concatenate([field_re, field_im], axis=1)


def unmix_rows(mixed_grad, kernel):
    kernel_taps = kernel.shape[0]
    half_freq = kernel.shape[1] // 2
    grad_re = mixed_grad[:, :half_freq]
    grad_im = mixed_grad[:, half_freq:]
    summed = None
    for offset in range(kernel_taps):
        kern_re = kernel[offset, :half_freq]
        kern_im = kernel[offset, half_freq:]
        back_re = grad_re * kern_re + grad_im * kern_im
        back_im = grad_im * kern_re - grad_re * kern_im
        padded = jnp.pad(
            jnp.concatenate([back_re, back_im], axis=1),
            ((offset, kernel_taps - 1 - offset), (0, 0)),
        )
        summed = padded if summed is None else summed + padded
    return summed


def image_kernels(extended, kernel_set, selectors, inverse_low, columns, focus_count):
    row_count = extended.shape[0] - kernel_set.shape[1] + 1

    def advance(summed, items):
        kernel, selector = items
        mixed = mix_rows(extended, kernel).astype(jnp.bfloat16)
        fields = jnp.dot(mixed, inverse_low, preferred_element_type=jnp.float32)
        energy = fields[:, :columns] ** 2 + fields[:, columns:] ** 2
        return (summed + selector[:, None, None] * energy[None], fields)

    start_sum = jnp.zeros((focus_count, row_count, columns), jnp.float32)
    return lax.scan(advance, start_sum, (kernel_set, selectors))


def adjoint(kernel_set, field_set, selectors, inverse_low, aerial_grads, ext_grad):

    def advance_back(summed, items):
        kernel, fields, selector = items
        aerial_grad = jnp.tensordot(selector, aerial_grads, axes=1)
        doubled = 2.0 * jnp.concatenate([aerial_grad, aerial_grad], axis=1)
        field_grad = (doubled * fields).astype(jnp.bfloat16)
        mixed_grad = lax.dot_general(
            field_grad, inverse_low, (((1,), (1,)), ((), ())), preferred_element_type=jnp.float32
        )
        return (summed + unmix_rows(mixed_grad, kernel), None)

    return lax.scan(advance_back, ext_grad, (kernel_set, field_set, selectors))[0]


def per_device(mask_logits, target, kernels, dose_levels):
    row_count = mask_logits.shape[0]
    columns = mask_logits.shape[1]
    focus_count = kernels.shape[0]
    kernel_count = kernels.shape[1]
    dose_count = dose_levels.shape[0]
    corner_total = focus_count * dose_count
    half_freq = kernels.shape[3] // 2
    rim_rows = kernels.shape[2] // 2
    forward, inverse = dft_tables(columns, half_freq)
    forward_low = forward.astype(jnp.bfloat16)
    inverse_low = inverse.astype(jnp.bfloat16)
    mask_field = jnp.tanh(mask_logits)
    mask_low = mask_field.astype(jnp.bfloat16)
    spectra = jnp.dot(mask_low, forward_low, preferred_element_type=jnp.float32).astype(
        jnp.bfloat16
    )
    extended = extended_2(spectra, (("tile", 0),), rim_rows)
    extended = extended.astype(jnp.float32)
    focus_ids = jnp.arange(focus_count, dtype=jnp.int32)
    dose_ids = jnp.arange(dose_count, dtype=jnp.int32)
    share_cols = columns // lax.axis_size("corner")
    offset_col = lax.axis_index("corner") * share_cols
    ext_grad = jnp.zeros(extended.shape, jnp.float32)
    corners_here = corner_total // lax.axis_size("corner")
    first_corner = lax.axis_index("corner") * corners_here
    single = jnp.ones((kernel_count, 1), jnp.float32)
    picked_sets = []
    field_sets = []
    dose_values = []
    resists = []
    soft_high = jnp.zeros((row_count, columns), jnp.float32)
    soft_low = jnp.zeros((row_count, columns), jnp.float32)
    for corner in range(corners_here):
        global_corner = first_corner + corner
        chosen = (focus_ids == global_corner // dose_count)[:, None, None, None]
        picked = jnp.sum(jnp.where(chosen, kernels, 0.0), axis=0)
        dose_value = jnp.sum(jnp.where(dose_ids == global_corner % dose_count, dose_levels, 0.0))
        stacked, field_set = image_kernels(extended, picked, single, inverse_low, columns, 1)
        aerial = stacked[0]
        resist = jax.nn.sigmoid(STEEPNESS * (dose_value * aerial - THRESHOLD))
        picked_sets.append(picked)
        field_sets.append(field_set)
        dose_values.append(dose_value)
        resists.append(resist)
        soft_high = soft_high + jnp.exp(SHARPNESS * resist)
        soft_low = soft_low + jnp.exp(-SHARPNESS * resist)
    high_total, low_total = (
        lax.psum(soft_high.astype(jnp.bfloat16), "corner").astype(jnp.float32),
        lax.psum(soft_low.astype(jnp.bfloat16), "corner").astype(jnp.float32),
    )
    wanted = target.astype(jnp.float32)
    top_band = jnp.log(high_total) / SHARPNESS
    bottom_band = -jnp.log(low_total) / SHARPNESS
    pv_share = lax.dynamic_slice_in_dim(top_band - bottom_band, offset_col, share_cols, 1)
    high_weight = (top_band - wanted) / high_total
    low_weight = (bottom_band - wanted) / low_total
    for corner in range(corners_here):
        resist = resists[corner]
        resist_grad = high_weight * jnp.exp(SHARPNESS * resist) + low_weight * jnp.exp(
            -SHARPNESS * resist
        )
        aerial_grad = resist_grad * STEEPNESS * dose_values[corner] * resist * (1.0 - resist)
        ext_grad = adjoint(
            picked_sets[corner],
            field_sets[corner],
            single,
            inverse_low,
            aerial_grad[None],
            ext_grad,
        )
    upper_rim = ext_grad[:rim_rows]
    lower_rim = ext_grad[rim_rows + row_count :]
    inner = ext_grad[rim_rows : rim_rows + row_count]
    from_below = passed_along(upper_rim, "tile", -1)
    from_above = passed_along(lower_rim, "tile", 1)
    inner = inner.at[row_count - rim_rows :].add(from_below)
    inner = inner.at[:rim_rows].add(from_above)
    full_grad = lax.dot_general(
        inner,
        forward,
        (((1,), (1,)), ((), ())),
        precision=lax.Precision.HIGHEST,
        preferred_element_type=jnp.float32,
    )
    mask_grad = lax.psum_scatter(
        full_grad.astype(jnp.bfloat16), "corner", scatter_dimension=1, tiled=True
    ).astype(jnp.float32)
    mask_share = lax.dynamic_slice_in_dim(mask_field, offset_col, share_cols, 1)
    return (pv_share, mask_grad * (1.0 - mask_share**2))


def solution(mesh):
    return jax.shard_map(
        per_device,
        mesh=mesh,
        in_specs=(P("tile", None), P("tile", None), P(), P()),
        out_specs=(P("tile", "corner"), P("tile", "corner")),
        check_vma=False,
    )
```

profile of v0, /device:TPU:2, one launch (start us, length us, event | category | flops | bytes accessed | tf_op | source)
XLA Modules:
  0.0 646.2 jit_solution(12291831019727170649)
XLA Ops:
  7.2 4.2 cosine_multiply_fusion
  13.4 1.9 collective-permute-start
  15.3 7.4 %collective-permute-start.1 = (bf16[12,384]{1,0:T(8,128)(2,1)}, bf16[12,384]{1,0:T(8,128)(2,1)}, u32[]{:S(2)}, u32[]{:S(2)}) collective-permute-start(bf16[12,384]{1,0:T(8,128)(2,1)} %get-tuple-element.752), channel_id=1, source_target_pairs={{8,0},{16,8},{24,16},{32,24},{40,32},{48,40},{56,48},{64,56},{72,6... | collective-permute-start | bytes 27656 | tf_op jit(solution)/shard_map/ppermute | solution.py:21
  22.7 3.7 fusion.139
  26.5 3.2 select_reduce_fusion
  32.0 6.2 broadcast.250.clone.1
  38.2 79.1 %while.55 = (s32[]{:T(128)}, f32[1,128,1024]{2,1,0:T(8,128)}, f32[12,128,2048]{2,1,0:T(8,128)}, f32[152,384]{1,0:T(8,128)S(1)}, f32[12,25,384]{2,1,0:T(8,128)}, ...) while((s32[]{:T(128)}, f32[1,128,1024]{2,1,0:T(8,128)}, f32[12,128,2048]{2,1,0:T(8,128)}, ...), condition=%wide.region_7.8_spmd.clone, body=%wide.region_6.7_spmd.clone.sunk | while | flops 207093760 | bytes 16025187 | solution.py:99
  48.5 2.0 fusion.214
  55.2 2.0 fusion.214
  61.8 2.0 fusion.214
  68.5 2.0 fusion.214
  75.2 2.0 fusion.214
  81.9 2.0 fusion.214
  88.6 2.0 fusion.214
  95.2 2.0 fusion.214
  101.9 2.0 fusion.214
  108.6 2.0 fusion.214
  115.3 2.0 fusion.214
  117.3 6.1 broadcast.250.clone
  123.4 59.8 %while.54 = (s32[]{:T(128)}, f32[1,128,1024]{2,1,0:T(8,128)S(1)}, f32[12,128,2048]{2,1,0:T(8,128)}, f32[152,384]{1,0:T(8,128)S(1)}, f32[12,25,384]{2,1,0:T(8,128...) while((s32[]{:T(128)}, f32[1,128,1024]{2,1,0:T(8,128)S(1)}, ...), condition=%wide.region_3.4_spmd.clone, body=%wide.region_2.3_spmd.clone.sunk | while | flops 207093760 | bytes 16025187 | solution.py:99
  183.2 3.8 add_convert_fusion.5
  188.5 89.9 %all-reduce.53.cloned.1.call-done = (bf16[128,1024]{1,0:T(8,128)(2,1)}, bf16[128,1024]{1,0:T(8,128)(2,1)}) async-done(((bf16[128,1024]{1,0:T(8,128)(2,1)}, bf16[128,1024]{1,0:T(8,128)(2,1)}), (bf16[128,1024]{1,0:T(8,128)(2,1)}, bf16[128,1024]{1,0:T(8,128)(2,1)})) %all-reduce.53.cloned.1.call-update) | async-done | bytes 524304 | tf_op jit(solution)/shard_map/psum | solution.py:166
  278.4 4.3 fusion.145
  282.8 191.4 %while.56 = (s32[]{:T(128)}, f32[152,384]{1,0:T(8,128)S(1)}, f32[128,2048]{1,0:T(8,128)S(1)}, f32[12,128,2048]{2,1,0:T(8,128)}, bf16[384,2048]{1,0:T(8,128)(2,1)...) while((s32[]{:T(128)}, f32[152,384]{1,0:T(8,128)S(1)}, f32[128,2048]{1,0:T(8,128)S(1)}, ...), condition=%wide.region_11.12_spmd.clone, body=%wide.region_10.11_spmd.clone.sunk | while | flops 215838720 | bytes 16126051 | solution.py:114
  283.7 1.9 fusion.218
  294.4 4.4 fusion.221
  299.7 1.9 fusion.218
  310.3 4.4 fusion.221
  315.6 1.9 fusion.218
  326.3 4.4 fusion.221
  331.6 1.9 fusion.218
  342.2 4.4 fusion.221
  347.5 1.9 fusion.218
  358.2 4.4 fusion.221
  363.5 1.9 fusion.218
  374.1 4.4 fusion.221
  379.4 1.9 fusion.218
  390.1 4.4 fusion.221
  395.4 1.9 fusion.218
  406.0 4.4 fusion.221
  411.3 1.9 fusion.218
  422.0 4.4 fusion.221
  427.3 1.9 fusion.218
  437.9 4.4 fusion.221
  443.2 1.9 fusion.218
  453.9 4.4 fusion.221
  459.2 1.9 fusion.218
  469.8 4.4 fusion.221
  475.5 76.4 %while.53 = (s32[]{:T(128)}, f32[152,384]{1,0:T(8,128)S(1)}, f32[128,2048]{1,0:T(8,128)S(1)}, f32[12,128,2048]{2,1,0:T(8,128)}, bf16[384,2048]{1,0:T(8,128)(2,1)S(1)}, /*index=5*/f32[12,25,384]{2,1,0:T(8,128)}, s32[]{:T(128)}) while((s32[]{:T(128)}, f32[152,384]{1,0:T(8,128)S(1)}, f32[128,2048]{1,0:T(8,128)S(1)}, ...), condition=%wide.region_13.14_spmd, body=%wide.region_12.13_spmd.sunk | while | flops 215780352 | bytes 16126033 | solution.py:114
  482.8 1.9 fusion.201
  489.1 1.9 fusion.201
  495.5 1.9 fusion.201
  501.9 1.9 fusion.201
  508.3 1.9 fusion.201
  514.6 1.9 fusion.201
  521.0 1.9 fusion.201
  527.4 1.9 fusion.201
  533.7 1.9 fusion.201
  546.5 1.9 fusion.201
  552.0 1.9 collective-permute-start.2
  553.9 2.5 collective-permute-start.3
  556.7 5.1 collective-permute-done.3
  562.1 3.4 convolution_convert_fusion
  567.9 69.9 %reduce-scatter.4.cloned.1.call-done = bf16[128,128]{1,0:T(8,128)(2,1)} async-done(((bf16[1024,128]{1,0:T(8,128)(2,1)}), bf16[128,128]{1,0:T(8,128)(2,1)}) %reduce-scatter.4.cloned.1.call-update) | async-done | bytes 32784
  (555 shorter events, 299.3 us)
Async XLA Ops:
  7.2 5.2 copy-start.3
  7.2 271.2 %all-reduce.53.cloned.1.call-start = ((), (), s32[]{:S(2)}) async-start(), calls=%async_computation.2 | async-start | bytes 1048576 | tf_op jit(solution)/shard_map/psum | solution.py:166
  11.4 1.0 copy-start.1
  11.4 1.4 copy-start.2
  12.4 14.1 %copy-start.5 = (f32[4,12,25,384]{3,0,2,1:T(4,128)S(1)}, f32[4,12,25,384]{3,0,2,1:T(4,128)}, u32[]{:S(2)}) copy-start(f32[4,12,25,384]{3,0,2,1:T(4,128)} %param.18) | copy-start | bytes 5529604
  12.8 0.6 copy-start.7
  13.4 17.6 %collective-permute-start = (bf16[12,384]{1,0:T(8,128)(2,1)}, bf16[12,384]{1,0:T(8,128)(2,1)}, u32[]{:S(2)}, u32[]{:S(2)}) collective-permute-start(bf16[12,384]{1,0:T(8,128)(2,1)} %get-tuple-element.751), channel_id=1, source_target_pairs={{0,8},{8,16},{16,24},{24,32},{32,40},{40,48},{48,56},{56,64},{64,7... | collective-permute-start | bytes 27656 | tf_op jit(solution)/shard_map/ppermute | solution.py:20
  15.3 15.7 %collective-permute-start.1 = (bf16[12,384]{1,0:T(8,128)(2,1)}, bf16[12,384]{1,0:T(8,128)(2,1)}, u32[]{:S(2)}, u32[]{:S(2)}) collective-permute-start(bf16[12,384]{1,0:T(8,128)(2,1)} %get-tuple-element.752), channel_id=1, source_target_pairs={{8,0},{16,8},{24,16},{32,24},{40,32},{48,40},{56,48},{64,56},{72,6... | collective-permute-start | bytes 27656 | tf_op jit(solution)/shard_map/ppermute | solution.py:21
  29.8 0.7 copy-start.8
  183.2 95.2 %copy-start = (f32[1,128,1024]{2,1,0:T(8,128)S(1)}, f32[1,128,1024]{2,1,0:T(8,128)}, u32[]{:S(2)}) copy-start(f32[1,128,1024]{2,1,0:T(8,128)} %get-tuple-element.253) | copy-start | bytes 1572868
  183.2 95.2 %copy-start.6 = (s32[128,1024]{1,0:T(8,128)S(1)}, s32[128,1024]{1,0:T(8,128)}, u32[]{:S(2)}) copy-start(s32[128,1024]{1,0:T(8,128)} %param.17) | copy-start | bytes 1572868
  187.0 450.8 %reduce-scatter.4.cloned.1.call-start = ((), (), s32[]{:S(2)}) async-start(), calls=%async_computation.1 | async-start | bytes 294912
  552.0 4.5 collective-permute-start.2
  553.9 12.4 %copy-start.4 = (f32[128,1024]{1,0:T(8,128)S(1)}, f32[128,1024]{1,0:T(8,128)}, u32[]{:S(2)}) copy-start(f32[128,1024]{1,0:T(8,128)} %param.16) | copy-start | bytes 1572868
  553.9 7.8 %collective-permute-start.3 = (f32[12,384]{1,0:T(8,128)S(1)}, f32[12,384]{1,0:T(8,128)S(1)}, u32[]{:S(2)}, u32[]{:S(2)}) collective-permute-start(f32[12,384]{1,0:T(8,128)S(1)} %get-tuple-element.749), channel_id=1, source_target_pairs={{0,8},{8,16},{16,24},{24,32},{32,40},{40,48},{48,56},{56,64},{64,7... | collective-permute-start | bytes 55304 | tf_op jit(solution)/shard_map/ppermute | solution.py:29
Sparse Core Ops, SparseCore 0:
  187.1 91.2 all-reduce.52
  566.4 71.3 reduce-scatter.3
where the time goes:
time: 651 us; the launch traced here: 646 us
  other arithmetic  298 us (46%)
  waiting for transfers between devices  165 us (25%)
  matrix products  84.2 us (13%)
  local copies, waits for them, and re-layouts  67.4 us (10%)
  between operations  15.6 us (2%)
  starting transfers between devices  14 us (2%)
    add x216, other arithmetic, unmix_rows(): back_re = grad_re * kern_re + grad_im * kern_im  123 us
    psum x1, waiting for transfers between devices, per_device(): lax.psum(soft_low.astype(jnp.bfloat16), 'corner').astype(jnp.float32)  89.9 us
    add x24, other arithmetic, advance_back(): return (summed + unmix_rows(mixed_grad, kernel), None)  73.1 us
    unnamed x3, waiting for transfers between devices  70 us
    another operation x49, other arithmetic  54.7 us
    dot_general x24, matrix products, advance_back(): lax.dot_general(field_grad, inverse_low, (((1,), (1,)), ((), ())), prefer...  44.7 us
    squeeze x48, local copies, waits for them, and re-layouts, image_kernels(): return lax.scan(advance, start_sum, (kernel_set, selectors))  38.6 us
    dot_general x24, matrix products, advance(): fields = jnp.dot(mixed, inverse_low, preferred_element_type=jnp.float32)  35.7 us
  transfers between devices with their start and end apart: 6, of which 3 were waited for; matrix products, arithmetic and copies ran while one was open for 1% of the time, Pallas kernels for 0%

commit v1 on v0

v1 whole, which is shorter than its diff:
```python
import math

import jax
import jax.numpy as jnp
import numpy as np
from jax import lax
from jax.experimental import pallas as pl
from jax.experimental.pallas import tpu as pltpu
from jax.sharding import PartitionSpec as P

STEEPNESS = 4.0
THRESHOLD = 1.0
SHARPNESS = 12.0

BF = jnp.bfloat16
F32 = jnp.float32

W = 1024
NF = 192
LANES = 256
TAPS = 25
RIM = TAPS // 2
ROWS = 128
NK = 12
NFOC = 4
NDOSE = 4
SHARE = 19
PAIR = 20
U = 48
GRID = 384
EDGE = 32
TEDGE = 16
MSG = 48 + 32
TURN = 1.62425


def low(table):
    return jnp.asarray(np.asarray(table, np.float32)).astype(BF)


def low_parts(table):
    table = np.asarray(table, np.float32)
    high = table.astype(jnp.bfloat16)
    return jnp.asarray(high), jnp.asarray((table - high.astype(np.float32)).astype(jnp.bfloat16))


def forward_table():
    phase = np.outer(np.arange(NF) - NF // 2, np.arange(W)) % W
    angle = 2.0 * math.pi * phase / W
    scale = 1.0 / math.sqrt(W)
    table = np.zeros((W, 2 * LANES))
    table[:, :NF] = scale * np.cos(angle).T
    table[:, LANES : LANES + NF] = -scale * np.sin(angle).T
    return table


def inverse_table():
    phase = np.outer(np.arange(NF) - NF // 2, np.arange(GRID)) % GRID
    angle = 2.0 * math.pi * phase / GRID
    scale = 1.0 / math.sqrt(W)
    table = np.zeros((2 * LANES, 2 * GRID))
    table[:NF, :GRID] = scale * np.cos(angle)
    table[:NF, GRID:] = scale * np.sin(angle)
    table[LANES : LANES + NF, :GRID] = -scale * np.sin(angle)
    table[LANES : LANES + NF, GRID:] = scale * np.cos(angle)
    return table


def interpolation_table():
    where = np.arange(W)[None, :] / W - np.arange(GRID)[:, None] / GRID
    orders = np.arange(1, NF)
    table = np.ones((GRID, W))
    for order in orders:
        table += 2.0 * np.cos(2.0 * math.pi * order * where)
    return table / GRID


def row_angles(left, right):
    return 2.0 * math.pi * (np.outer(np.arange(left), np.arange(right)) % U) / U


def tap_table(count=4):
    angle = row_angles(U, TAPS)
    table = np.zeros((count * U, count * 64))
    for q in range(count):
        table[q * U : (q + 1) * U, q * 64 : q * 64 + TAPS] = np.cos(angle)
        table[q * U : (q + 1) * U, q * 64 + 32 : q * 64 + 32 + TAPS] = np.sin(angle)
    return TURN * table


def window_table():
    angle = row_angles(U, U)
    return TURN * np.concatenate([np.cos(angle), -np.sin(angle)], axis=1)


def back_table():
    angle = row_angles(U, U)
    return TURN * np.concatenate([np.cos(angle), np.sin(angle)], axis=1)


def mix_table(count=2):
    angle = row_angles(PAIR, U)
    table = np.zeros((count * PAIR, count * 2 * U))
    for q in range(count):
        rows = slice(q * PAIR, (q + 1) * PAIR)
        table[rows, q * 2 * U : q * 2 * U + U] = np.cos(angle)
        table[rows, q * 2 * U + U : (q + 1) * 2 * U] = np.sin(angle)
    return TURN * table


def unmix_table(count=4):
    angle = row_angles(U, PAIR)
    half = count * PAIR
    table = np.zeros((count * U, 2 * half))
    for q in range(count):
        rows = slice(q * U, (q + 1) * U)
        table[rows, q * PAIR : (q + 1) * PAIR] = np.cos(angle)
        table[rows, half + q * PAIR : half + (q + 1) * PAIR] = -np.sin(angle)
    return TURN * table


def dot(left, right):
    return jnp.dot(left, right, preferred_element_type=F32)


def dot_nt(left, right):
    return lax.dot_general(left, right, (((1,), (1,)), ((), ())), preferred_element_type=F32)


def turned(value):
    value = value.astype(BF)
    swapped = jnp.concatenate([-value[:, LANES:], value[:, :LANES]], axis=1)
    return jnp.concatenate([value, swapped], axis=0)


def picked(count, length, first):
    row = lax.broadcasted_iota(jnp.int32, (count, length), 0) + first
    row = jnp.where(row >= length, row - length, row)
    column = lax.broadcasted_iota(jnp.int32, (count, length), 1)
    return jnp.where(row == column, 1.0, 0.0).astype(BF)


def edge_kernel(mask_ref, target_ref, out_ref, mask_rows, target_rows, sems):
    down = lax.axis_index("corner") < lax.axis_size("corner") // 2
    mask_from = pl.multiple_of(jnp.where(down, ROWS - EDGE, 0), EDGE)
    target_from = pl.multiple_of(jnp.where(down, ROWS - TEDGE, 0), TEDGE)
    copies = [
        pltpu.make_async_copy(mask_ref.at[pl.ds(mask_from, EDGE)], mask_rows, sems.at[0]),
        pltpu.make_async_copy(target_ref.at[pl.ds(target_from, TEDGE)], target_rows, sems.at[1]),
    ]
    for copy in copies:
        copy.start()
    for copy in copies:
        copy.wait()
    out_ref[:EDGE] = jnp.tanh(mask_rows[...]).astype(BF)
    out_ref[EDGE:] = target_rows[...].astype(F32).astype(BF)


def prepare_kernel(kernels_ref, mask_ref, forward_ref, tap_ref, hat_ref, spectra_ref, slope_ref, stack_ref):
    stack_ref[...] = jnp.zeros_like(stack_ref)
    for group in range(NFOC * NK // 4):
        slot = group % 2
        for q in range(4):
            taps = kernels_ref[group * 4 + q]
            re = taps[:, :NF]
            im = taps[:, NF:]
            base = q * 64
            stack_ref[slot, base : base + TAPS, :NF] = re
            stack_ref[slot, base : base + TAPS, LANES : LANES + NF] = im
            stack_ref[slot, base + 32 : base + 32 + TAPS, :NF] = -im
            stack_ref[slot, base + 32 : base + 32 + TAPS, LANES : LANES + NF] = re
        hat = dot(tap_ref[...], stack_ref[slot].astype(BF)).astype(BF)
        hat_ref[group * 4 : group * 4 + 4] = hat.reshape(4, U, 2 * LANES)
    field = jnp.tanh(mask_ref[...])
    spectra_ref[...] = dot(field.astype(BF), forward_ref[...]).astype(BF)
    column = pl.multiple_of(lax.axis_index("corner") * ROWS, ROWS)
    share = jnp.tanh(mask_ref[:, pl.ds(column, ROWS)])
    slope_ref[...] = 1.0 - share * share


def image_kernel(
    dose_ref,
    edge_ref,
    spectra_ref,
    target_ref,
    hat_ref,
    forward_ref,
    inverse_ref,
    interp_ref,
    interp_low_ref,
    window_ref,
    mix_ref,
    unmix_ref,
    back_ref,
    out_ref,
    mixed_ref,
    field_ref,
    aerial_ref,
    grad_ref,
    fold_ref,
    band_ref,
):
    corner = lax.axis_index("corner")
    tile = lax.axis_index("tile")
    edge = dot(edge_ref[:EDGE], forward_ref[...]).astype(BF)
    rows = jnp.concatenate([edge, spectra_ref[...]], axis=0)
    pick = picked(U, ROWS + EDGE, SHARE * corner + (EDGE - 2 * RIM))
    mask_hat = dot(window_ref[...], turned(dot(pick, rows))) * (1.0 / (TURN * TURN * TURN * U))
    mask_re = mask_hat[:, :LANES]
    mask_im = mask_hat[:, LANES:]
    for group in range(NFOC * NK // 4):
        parts = []
        for pair in range(2):
            stack = []
            for q in range(2):
                hat = hat_ref[group * 4 + pair * 2 + q].astype(F32)
                hat_re = hat[:, :LANES]
                hat_im = hat[:, LANES:]
                re = (mask_re * hat_re - mask_im * hat_im).astype(BF)
                im = (mask_re * hat_im + mask_im * hat_re).astype(BF)
                stack.append(jnp.concatenate([re, im], axis=1))
                stack.append(jnp.concatenate([-im, re], axis=1))
            parts.append(dot(mix_ref[...], jnp.concatenate(stack, axis=0)))
        mixed_ref[group * 4 * PAIR : (group + 1) * 4 * PAIR] = jnp.concatenate(parts, axis=0).astype(BF)
    per_focus = NK * PAIR
    fold_ref[...] = jnp.zeros_like(fold_ref)
    for focus in range(NFOC):
        fields = dot(mixed_ref[focus * per_focus : (focus + 1) * per_focus], inverse_ref[...])
        field_ref[focus * per_focus : (focus + 1) * per_focus] = fields
        power = fields[:, :GRID] * fields[:, :GRID] + fields[:, GRID:] * fields[:, GRID:]
        summed = power[: 2 * PAIR]
        for pair in range(1, NK // 2):
            summed = summed + power[pair * 2 * PAIR : (pair + 1) * 2 * PAIR]
        fold_ref[focus, : 2 * PAIR] = summed
        aerial_ref[focus * 24 : (focus + 1) * 24, :GRID] = (
            fold_ref[focus, 0:24] + fold_ref[focus, PAIR : PAIR + 24]
        )
    coarse = aerial_ref[:, :GRID]
    coarse_high = coarse.astype(BF)
    coarse_low = (coarse - coarse_high.astype(F32)).astype(BF)
    both = dot(jnp.concatenate([coarse_high, coarse_low], axis=0), interp_ref[...])
    aerial_ref[...] = both[: NFOC * 24] + both[NFOC * 24 :] + dot(coarse_high, interp_low_ref[...])
    wanted_rows = jnp.concatenate([edge_ref[EDGE:], target_ref[...].astype(F32).astype(BF)], axis=0)
    pick = picked(24, ROWS + TEDGE, SHARE * corner + (TEDGE - RIM))
    band_ref[...] = dot(pick, wanted_rows)
    local = lax.broadcasted_iota(jnp.int32, (24, ROWS), 0)
    pixel = tile * ROWS + SHARE * corner - RIM + local
    valid = (local < SHARE) & (pixel >= 0) & (pixel < ROWS * lax.axis_size("tile"))
    valid = jnp.where(valid, 1.0, 0.0)
    doses = [dose_ref[d] for d in range(NDOSE)]
    for chunk in range(W // ROWS):
        cols = slice(chunk * ROWS, (chunk + 1) * ROWS)
        high = None
        low_sum = None
        kept = []
        for focus in range(NFOC):
            aerial = aerial_ref[focus * 24 : (focus + 1) * 24, cols]
            for d in range(NDOSE):
                level = (0.5 * STEEPNESS * doses[d]) * aerial - 0.5 * STEEPNESS * THRESHOLD
                resist = 0.5 * jnp.tanh(level) + 0.5
                up = jnp.exp(SHARPNESS * resist)
                down = jnp.exp(-SHARPNESS * resist)
                high = up if high is None else high + up
                low_sum = down if low_sum is None else low_sum + down
                kept.append((resist, up, down))
        wanted = band_ref[:, cols]
        top = jnp.log(high) / SHARPNESS
        bottom = -jnp.log(low_sum) / SHARPNESS
        band_ref[:, cols] = top - bottom
        high_weight = valid * (top - wanted) / high
        low_weight = valid * (bottom - wanted) / low_sum
        for focus in range(NFOC):
            total = None
            for d in range(NDOSE):
                resist, up, down = kept[focus * NDOSE + d]
                term = (high_weight * up + low_weight * down) * (resist * (1.0 - resist))
                term = term * (2.0 * STEEPNESS * doses[d])
                total = term if total is None else total + term
            grad_ref[focus * 24 : (focus + 1) * 24, cols] = total
    coarse_grad = dot_nt(grad_ref[...].astype(BF), interp_ref[...])
    acc_re = jnp.zeros((U, LANES), F32)
    acc_im = jnp.zeros((U, LANES), F32)
    for focus in range(NFOC):
        part = coarse_grad[focus * 24 : (focus + 1) * 24]
        fold_ref[focus, 0:24] = part
        fold_ref[focus, PAIR : PAIR + 24] = part
        twice = fold_ref[focus, : 2 * PAIR]
        twice = jnp.concatenate([twice, twice], axis=1)
        twice = jnp.concatenate([twice, twice], axis=0)
        for group in range(NK // 4):
            start = focus * per_focus + group * 4 * PAIR
            field_grad = (twice * field_ref[start : start + 4 * PAIR]).astype(BF)
            mixed_grad = dot_nt(field_grad, inverse_ref[...])
            hats = dot(unmix_ref[...], turned(mixed_grad))
            for q in range(4):
                grad_re = hats[q * U : (q + 1) * U, :LANES]
                grad_im = hats[q * U : (q + 1) * U, LANES:]
                hat = hat_ref[focus * NK + group * 4 + q].astype(F32)
                hat_re = hat[:, :LANES]
                hat_im = hat[:, LANES:]
                acc_re = acc_re + (grad_re * hat_re + grad_im * hat_im)
                acc_im = acc_im + (grad_im * hat_re - grad_re * hat_im)
    acc = jnp.concatenate([acc_re, acc_im], axis=1) * (1.0 / (TURN * TURN * TURN * U))
    spectra_grad = dot(back_ref[...], turned(acc))
    mask_grad = dot_nt(spectra_grad.astype(BF), forward_ref[...]).astype(BF)
    for block in range(W // ROWS):
        cols = slice(block * ROWS, (block + 1) * ROWS)
        out_ref[block, :U] = mask_grad[:, cols]
        band = jnp.concatenate([band_ref[:, cols], jnp.zeros((8, ROWS), F32)], axis=0)
        out_ref[block, U:] = band.astype(BF)


def finish_kernel(blocks_ref, slope_ref, band_ref, grad_ref, sum_ref, rows_ref):
    sum_ref[...] = jnp.zeros_like(sum_ref)
    for source in range(blocks_ref.shape[0]):
        block = blocks_ref[source].astype(F32)
        start = SHARE * source
        sum_ref[start : start + U] = sum_ref[start : start + U] + block[:U]
        rows_ref[start : start + 24] = block[U : U + 24]
    grad_ref[...] = sum_ref[2 * RIM : 2 * RIM + ROWS] * slope_ref[...]
    band_ref[...] = rows_ref[RIM : RIM + ROWS]


def params(mib):
    return pltpu.CompilerParams(vmem_limit_bytes=mib << 20)


def whole(count):
    return [pl.BlockSpec(memory_space=pltpu.VMEM)] * count


def per_device(mask_logits, target, kernels, dose_levels):
    tiles = lax.axis_size("tile")
    corners = lax.axis_size("corner")
    edge = pl.pallas_call(
        edge_kernel,
        name="edge",
        out_shape=jax.ShapeDtypeStruct((EDGE + TEDGE, W), BF),
        in_specs=[pl.BlockSpec(memory_space=pl.ANY)] * 2,
        out_specs=pl.BlockSpec(memory_space=pltpu.VMEM),
        scratch_shapes=[
            pltpu.VMEM((EDGE, W), F32),
            pltpu.VMEM((TEDGE, W), jnp.int32),
            pltpu.SemaphoreType.DMA((2,)),
        ],
    )(mask_logits, target)
    pairs = []
    for i in range(tiles - 1):
        for c in range(corners):
            begin = SHARE * c - 2 * RIM
            if begin < 0:
                pairs.append((i * corners + c, (i + 1) * corners + c))
            elif begin + SHARE + 2 * RIM > ROWS:
                pairs.append(((i + 1) * corners + c, i * corners + c))
    edge = lax.ppermute(edge, ("tile", "corner"), pairs)
    forward = low(forward_table())
    inverse = low(inverse_table())
    interp, interp_low = low_parts(interpolation_table())
    count = NFOC * NK
    hats, spectra, slope = pl.pallas_call(
        prepare_kernel,
        name="prepare",
        out_shape=(
            jax.ShapeDtypeStruct((count, U, 2 * LANES), BF),
            jax.ShapeDtypeStruct((ROWS, 2 * LANES), BF),
            jax.ShapeDtypeStruct((ROWS, ROWS), F32),
        ),
        in_specs=whole(4),
        out_specs=tuple(whole(3)),
        scratch_shapes=[pltpu.VMEM((2, 256, 2 * LANES), F32)],
        compiler_params=params(24),
        cost_estimate=pl.CostEstimate(flops=2_000_000_000, bytes_accessed=8_000_000, transcendentals=0),
    )(kernels.reshape(count, TAPS, 2 * NF), mask_logits, forward, low(tap_table()))
    blocks = pl.pallas_call(
        image_kernel,
        name="image",
        out_shape=jax.ShapeDtypeStruct((W // ROWS, MSG, ROWS), BF),
        in_specs=[pl.BlockSpec(memory_space=pltpu.SMEM)] + whole(12),
        out_specs=pl.BlockSpec(memory_space=pltpu.VMEM),
        scratch_shapes=[
            pltpu.VMEM((count * PAIR, 2 * LANES), BF),
            pltpu.VMEM((count * PAIR, 2 * GRID), F32),
            pltpu.VMEM((NFOC * 24, W), F32),
            pltpu.VMEM((NFOC * 24, W), F32),
            pltpu.VMEM((NFOC, U, GRID), F32),
            pltpu.VMEM((24, W), F32),
        ],
        compiler_params=params(32),
        cost_estimate=pl.CostEstimate(flops=4_000_000_000, bytes_accessed=8_000_000, transcendentals=0),
    )(
        dose_levels,
        edge,
        spectra,
        target,
        hats,
        forward,
        inverse,
        interp,
        interp_low,
        low(window_table()),
        low(mix_table()),
        low(unmix_table()),
        low(back_table()),
    )
    blocks = lax.all_to_all(blocks, "corner", 0, 0, tiled=True)
    return pl.pallas_call(
        finish_kernel,
        name="finish",
        out_shape=(
            jax.ShapeDtypeStruct((ROWS, ROWS), F32),
            jax.ShapeDtypeStruct((ROWS, ROWS), F32),
        ),
        in_specs=whole(2),
        out_specs=tuple(whole(2)),
        scratch_shapes=[pltpu.VMEM((192, ROWS), F32), pltpu.VMEM((160, ROWS), F32)],
    )(blocks, slope)


def solution(mesh):
    return jax.shard_map(
        per_device,
        mesh=mesh,
        in_specs=(P("tile", None), P("tile", None), P(), P()),
        out_specs=(P("tile", "corner"), P("tile", "corner")),
        check_vma=False,
    )
```

time: 651 us -> 40.9 us (0.06)
  other arithmetic: 298 us -> 0 us
  waiting for transfers between devices: 165 us -> 3.46 us
  matrix products: 84.2 us -> 0 us
  local copies, waits for them, and re-layouts: 67.4 us -> 2.52 us
  blocking collectives: 0 us -> 16.2 us
  Pallas kernels: 0 us -> 15.7 us
  between operations: 15.6 us -> 0.85 us
  starting transfers between devices: 14 us -> 2.05 us
    add x266 -> x0, other arithmetic: 222 us -> none  [the longest x216 123 us: unmix_rows(): back_re = grad_re * kern_re + grad_im * kern_im]
    psum x1 -> x0, waiting for transfers between devices: 89.9 us -> none  [per_device(): lax.psum(soft_low.astype(jnp.bfloat16), 'corner').astype(jnp.float32)]
    dot_general x50 -> x0, matrix products: 84.2 us -> none  [the longest x24 44.7 us: advance_back(): lax.dot_general(field_grad, inverse_low, (((1,), (1,)), ((), ())), prefer...]
    unnamed x3 -> x0, waiting for transfers between devices: 70 us -> none
    another operation x49 -> x0, other arithmetic: 54.7 us -> none
    squeeze x48 -> x0, local copies, waits for them, and re-layouts: 38.6 us -> none  [image_kernels(): return lax.scan(advance, start_sum, (kernel_set, selectors))]
    all_to_all x0 -> x1, blocking collectives: none -> 16.2 us  [per_device(): blocks = lax.all_to_all(blocks, 'corner', 0, 0, tiled=True)]
    pallas_call x0 -> x4, Pallas kernels: none -> 15.7 us  [the longest x1 10.8 us: per_device(): pl.pallas_call(image_kernel, name='image', out_shape=jax.ShapeDtypeStruct...]
  transfers between devices with their start and end apart: 6 -> 1, of which waited for: 3 -> 1; matrix products, arithmetic and copies ran while one was open for 1% -> 4% of each run, Pallas kernels for 0% -> 4%
where the time goes in v1:
time: 40.9 us; the launch traced here: 40.7 us
  blocking collectives  16.2 us (40%)
  Pallas kernels  15.7 us (38%)
  waiting for transfers between devices  3.46 us (8%)
  local copies, waits for them, and re-layouts  2.52 us (6%)
  starting transfers between devices  2.05 us (5%)
  between operations  0.85 us (2%)
    all_to_all x1, blocking collectives, per_device(): blocks = lax.all_to_all(blocks, 'corner', 0, 0, tiled=True)  16.2 us
    pallas_call x1, Pallas kernels, per_device(): pl.pallas_call(image_kernel, name='image', out_shape=jax.ShapeDtypeStruct...  10.8 us
    ppermute x1, waiting for transfers between devices, per_device(): edge = lax.ppermute(edge, ('tile', 'corner'), pairs)  3.46 us
    unnamed x27, local copies, waits for them, and re-layouts  2.52 us
    ppermute x1, starting transfers between devices, per_device(): edge = lax.ppermute(edge, ('tile', 'corner'), pairs)  2.05 us
    pallas_call x1, Pallas kernels, per_device(): pl.pallas_call(prepare_kernel, name='prepare', out_shape=(jax.ShapeDtypeS...  1.69 us
    pallas_call x1, Pallas kernels, per_device(): pl.pallas_call(finish_kernel, name='finish', out_shape=(jax.ShapeDtypeStr...  1.6 us
    pallas_call x1, Pallas kernels, per_device(): pl.pallas_call(edge_kernel, name='edge', out_shape=jax.ShapeDtypeStruct((...  1.59 us
  transfers between devices with their start and end apart: 1, of which 1 were waited for; matrix products, arithmetic and copies ran while one was open for 4% of the time, Pallas kernels for 4%

profile of v1, /device:TPU:2, one launch (start us, length us, event | category | flops | bytes accessed | tf_op | source)
XLA Modules:
  0.0 40.7 jit_solution(13989920747180393221)
XLA Ops:
  0.6 1.6 %edge.1 = bf16[48,1024]{1,0:T(8,128)(2,1)} custom-call(f32[128,1024]{1,0:T(8,128)} %mask_ref.3, s32[128,1024]{1,0:T(8,128)} %target_ref.3), custom_call_target="tpu_custom_call" | custom-call | tf_op jit(solution)/shard_map/edge/pallas_call | solution.py:335
  2.2 0.0 copy-start
  2.2 0.0 copy-start.4
  2.2 0.0 copy-start.9
  2.3 2.1 %collective-permute-start = (bf16[48,1024]{1,0:T(8,128)(2,1)}, bf16[48,1024]{1,0:T(8,128)(2,1)S(1)}, u32[]{:S(2)}, u32[]{:S(2)}) collective-permute-start(bf16[48,1024]{1,0:T(8,128)(2,1)} %edge.1), channel_id=1, source_target_pairs={{0,8},{1,9},{14,6},{15,7},{8,16},{9,17},{22,14},{23,15},{16,24},{1... | collective-permute-start | bytes 294920 | tf_op jit(solution)/shard_map/ppermute | solution.py:355
  4.3 1.8 %copy.15 = f32[4,12,25,384]{3,2,1,0:T(8,128)S(1)} copy(f32[4,12,25,384]{3,0,2,1:T(4,128)} %param.15) | data formatting | bytes 3686400 | tf_op args[2]
  6.2 0.0 copy-done
  6.2 0.0 copy-done.4
  6.2 0.0 copy-done.9
  6.2 0.0 copy-start.1
  6.2 0.0 copy-start.3
  6.2 0.0 copy-start.5
  6.2 0.0 copy-start.6
  6.2 0.0 copy-start.7
  6.2 0.0 copy-start.8
  6.3 0.0 copy-start.10
  6.3 0.0 copy-start.11
  6.3 0.0 copy-start.12
  6.3 1.7 %prepare.1 = (bf16[48,48,512]{2,1,0:T(8,128)(2,1)S(1)}, bf16[128,512]{1,0:T(8,128)(2,1)S(1)}, f32[128,128]{1,0:T(8,128)S(1)}) custom-call(f32[48,25,384]{2,1,0:T(8,128)S(1)} %bitcast.1, f32[128,1024]{1,0:T(8,128)S(1)} %copy-done, bf16[1024,512]{1,0:T(8,128)(2,1)S(1)} %copy-done.4, bf16[192,256]{1,0:T(8,128)(2,1)S(1)} %copy-done.9), custom_call_target="tpu_custom_call" | custom-call | flops 2000000000 | bytes 8000000 | tf_op jit(solution)/shard_map/prepare/pallas_call | solution.py:360
  8.0 0.0 copy-start.2
  8.0 0.6 %copy-done.2 = f32[128,128]{1,0:T(8,128)} copy-done((f32[128,128]{1,0:T(8,128)}, f32[128,128]{1,0:T(8,128)S(1)}, u32[]{:S(2)}) %copy-start.2) | copy-done | bytes 65560
  8.6 3.5 %collective-permute-done.edge_ref = bf16[48,1024]{1,0:T(8,128)(2,1)S(1)} collective-permute-done((bf16[48,1024]{1,0:T(8,128)(2,1)}, bf16[48,1024]{1,0:T(8,128)(2,1)S(1)}, u32[]{:S(2)}, u32[]{:S(2)}) %collective-permute-start) | collective-permute-done | bytes 98336 | tf_op jit(solution)/shard_map/ppermute | solution.py:355
  12.1 0.0 copy-done.1
  12.1 0.0 copy-done.3
  12.1 0.0 copy-done.5
  12.1 0.0 copy-done.6
  12.1 0.0 copy-done.7
  12.1 0.0 copy-done.8
  12.1 0.0 copy-done.10
  12.1 0.0 copy-done.11
  12.1 0.0 copy-done.12
  12.1 10.8 %image.1 = bf16[8,80,128]{2,1,0:T(8,128)(2,1)S(1)} custom-call(f32[4]{0:T(128)S(1)} %copy-done.3, bf16[48,1024]{1,0:T(8,128)(2,1)S(1)} %collective-permute-done.edge_ref, bf16[128,512]{1,0:T(8,128)(2,1)S(1)} %get-tuple-element.5.spectra_ref, s32[128,1024]{1,0:T(8,128)S(1)} %copy-done.1, bf16[48,48,512]{2,1,0:T(8,128)(2,1)S(1)} %get-tuple-element.6.hat_ref, ...), custom_call_target="tpu_custom_call" | custom-call | flops 4000000000 | bytes 8000000 | tf_op jit(solution)/shard_map/image/pallas_call | solution.py:374
  22.9 16.2 %all_to_all.5.blocks_ref = bf16[8,80,128]{2,1,0:T(8,128)(2,1)} all-to-all(bf16[8,80,128]{2,1,0:T(8,128)(2,1)S(1)} %image.1), channel_id=1, replica_groups=mesh['tile'=32,'corner'=8] {'corner'}, dimensions={0} | all-to-all | bytes 327680 | tf_op jit(solution)/shard_map/all_to_all | solution.py:405
  39.1 1.6 %finish.1 = (f32[128,128]{1,0:T(8,128)}, f32[128,128]{1,0:T(8,128)}) custom-call(bf16[8,80,128]{2,1,0:T(8,128)(2,1)} %all_to_all.5.blocks_ref, f32[128,128]{1,0:T(8,128)} %copy-done.2), custom_call_target="tpu_custom_call" | custom-call | tf_op jit(solution)/shard_map/finish/pallas_call | solution.py:406
Async XLA Ops:
  2.2 3.9 %copy-start = (f32[128,1024]{1,0:T(8,128)S(1)}, f32[128,1024]{1,0:T(8,128)}, u32[]{:S(2)}) copy-start(f32[128,1024]{1,0:T(8,128)} %mask_ref.3) | copy-start | bytes 1572868
  2.2 3.9 %copy-start.4 = (bf16[1024,512]{1,0:T(8,128)(2,1)S(1)}, bf16[1024,512]{1,0:T(8,128)(2,1)}, u32[]{:S(2)}) copy-start(bf16[1024,512]{1,0:T(8,128)(2,1)} %constant.27.forward_ref) | copy-start | bytes 3145732
  2.2 3.9 %copy-start.9 = (bf16[192,256]{1,0:T(8,128)(2,1)S(1)}, bf16[192,256]{1,0:T(8,128)(2,1)}, u32[]{:S(2)}) copy-start(bf16[192,256]{1,0:T(8,128)(2,1)} %constant.28.tap_ref) | copy-start | bytes 294916
  2.3 9.8 %collective-permute-start = (bf16[48,1024]{1,0:T(8,128)(2,1)}, bf16[48,1024]{1,0:T(8,128)(2,1)S(1)}, u32[]{:S(2)}, u32[]{:S(2)}) collective-permute-start(bf16[48,1024]{1,0:T(8,128)(2,1)} %edge.1), channel_id=1, source_target_pairs={{0,8},{1,9},{14,6},{15,7},{8,16},{9,17},{22,14},{23,15},{16,24},{1... | collective-permute-start | bytes 294920 | tf_op jit(solution)/shard_map/ppermute | solution.py:355
  6.2 5.9 %copy-start.1 = (s32[128,1024]{1,0:T(8,128)S(1)}, s32[128,1024]{1,0:T(8,128)}, u32[]{:S(2)}) copy-start(s32[128,1024]{1,0:T(8,128)} %target_ref.3) | copy-start | bytes 1572868
  6.2 5.9 %copy-start.3 = (f32[4]{0:T(128)S(1)}, f32[4]{0:T(128)}, u32[]{:S(2)}) copy-start(f32[4]{0:T(128)} %dose_ref.1) | copy-start | bytes 52
  6.2 5.9 %copy-start.5 = (bf16[384,1024]{1,0:T(8,128)(2,1)S(1)}, bf16[384,1024]{1,0:T(8,128)(2,1)}, u32[]{:S(2)}) copy-start(bf16[384,1024]{1,0:T(8,128)(2,1)} %constant.20.clone.interp_ref) | copy-start | bytes 2359300
  6.2 5.9 %copy-start.6 = (bf16[384,1024]{1,0:T(8,128)(2,1)S(1)}, bf16[384,1024]{1,0:T(8,128)(2,1)}, u32[]{:S(2)}) copy-start(bf16[384,1024]{1,0:T(8,128)(2,1)} %constant.21.clone.interp_low_ref) | copy-start | bytes 2359300
  6.2 5.9 %copy-start.7 = (bf16[512,768]{1,0:T(8,128)(2,1)S(1)}, bf16[512,768]{1,0:T(8,128)(2,1)}, u32[]{:S(2)}) copy-start(bf16[512,768]{1,0:T(8,128)(2,1)} %constant.29.inverse_ref) | copy-start | bytes 2359300
  6.2 5.9 %copy-start.8 = (bf16[192,160]{1,0:T(8,128)(2,1)S(1)}, bf16[192,160]{1,0:T(8,128)(2,1)}, u32[]{:S(2)}) copy-start(bf16[192,160]{1,0:T(8,128)(2,1)} %constant.32.unmix_ref) | copy-start | bytes 184324
  6.3 5.9 %copy-start.10 = (bf16[40,192]{1,0:T(8,128)(2,1)S(1)}, bf16[40,192]{1,0:T(8,128)(2,1)}, u32[]{:S(2)}) copy-start(bf16[40,192]{1,0:T(8,128)(2,1)} %constant.31.mix_ref) | copy-start | bytes 46084
  6.3 5.9 %copy-start.11 = (bf16[48,96]{1,0:T(8,128)(2,1)S(1)}, bf16[48,96]{1,0:T(8,128)(2,1)}, u32[]{:S(2)}) copy-start(bf16[48,96]{1,0:T(8,128)(2,1)} %constant.30.window_ref) | copy-start | bytes 27652
  6.3 5.9 %copy-start.12 = (bf16[48,96]{1,0:T(8,128)(2,1)S(1)}, bf16[48,96]{1,0:T(8,128)(2,1)}, u32[]{:S(2)}) copy-start(bf16[48,96]{1,0:T(8,128)(2,1)} %constant.33.back_ref) | copy-start | bytes 27652
  8.0 0.6 %copy-start.2 = (f32[128,128]{1,0:T(8,128)}, f32[128,128]{1,0:T(8,128)S(1)}, u32[]{:S(2)}) copy-start(f32[128,128]{1,0:T(8,128)S(1)} %get-tuple-element.7.slope_ref) | copy-start | bytes 196612

commit v2 on v1

--- a/solution.py
+++ b/solution.py
@@ -26,6 +26,7 @@
 NDOSE = 4
 SHARE = 19
 PAIR = 20
+TAP_ROWS = 112
 U = 48
 GRID = 384
 EDGE = 32
@@ -36,12 +37,6 @@
 
 def low(table):
     return jnp.asarray(np.asarray(table, np.float32)).astype(BF)
-
-
-def low_parts(table):
-    table = np.asarray(table, np.float32)
-    high = table.astype(jnp.bfloat16)
-    return jnp.asarray(high), jnp.asarray((table - high.astype(np.float32)).astype(jnp.bfloat16))
 
 
 def forward_table():
@@ -79,13 +74,13 @@
     return 2.0 * math.pi * (np.outer(np.arange(left), np.arange(right)) % U) / U
 
 
-def tap_table(count=4):
+def tap_table():
     angle = row_angles(U, TAPS)
-    table = np.zeros((count * U, count * 64))
-    for q in range(count):
-        table[q * U : (q + 1) * U, q * 64 : q * 64 + TAPS] = np.cos(angle)
-        table[q * U : (q + 1) * U, q * 64 + 32 : q * 64 + 32 + TAPS] = np.sin(angle)
-    return TURN * table
+    table = np.zeros((NFOC, U, 2, TAP_ROWS))
+    for focus in range(NFOC):
+        table[focus, :, 0, focus : TAPS * NFOC : NFOC] = np.cos(angle)
+        table[focus, :, 1, focus : TAPS * NFOC : NFOC] = np.sin(angle)
+    return TURN * table.reshape(NFOC * U, 2 * TAP_ROWS)
 
 
 def window_table():
@@ -119,12 +114,23 @@
     return TURN * table
 
 
+def placing_tables(count):
+    grad = np.zeros((ROWS, count, U))
+    band = np.zeros((ROWS, count, MSG - U))
+    for source in range(count):
+        for row in range(SHARE + 2 * RIM):
+            pixel = SHARE * source + row - 2 * RIM
+            if 0 <= pixel < ROWS:
+                grad[pixel, source, row] = 1.0
+        for row in range(SHARE):
+            pixel = SHARE * source + row - RIM
+            if 0 <= pixel < ROWS:
+                band[pixel, source, row] = 1.0
+    return grad.reshape(ROWS, -1), band.reshape(ROWS, -1)
+
+
 def dot(left, right):
     return jnp.dot(left, right, preferred_element_type=F32)
-
-
-def dot_nt(left, right):
-    return lax.dot_general(left, right, (((1,), (1,)), ((), ())), preferred_element_type=F32)
 
 
 def turned(value):
@@ -140,13 +146,14 @@
     return jnp.where(row == column, 1.0, 0.0).astype(BF)
 
 
-def edge_kernel(mask_ref, target_ref, out_ref, mask_rows, target_rows, sems):
+def edge_kernel(mask_ref, target_ref, dose_ref, out_ref, dose_rows_ref, mask_rows, target_rows, doses, sems):
     down = lax.axis_index("corner") < lax.axis_size("corner") // 2
     mask_from = pl.multiple_of(jnp.where(down, ROWS - EDGE, 0), EDGE)
     target_from = pl.multiple_of(jnp.where(down, ROWS - TEDGE, 0), TEDGE)
     copies = [
         pltpu.make_async_copy(mask_ref.at[pl.ds(mask_from, EDGE)], mask_rows, sems.at[0]),
         pltpu.make_async_copy(target_ref.at[pl.ds(target_from, TEDGE)], target_rows, sems.at[1]),
+        pltpu.make_async_copy(dose_ref, doses, sems.at[2]),
     ]
     for copy in copies:
         copy.start()
@@ -154,28 +161,32 @@
         copy.wait()
     out_ref[:EDGE] = jnp.tanh(mask_rows[...]).astype(BF)
     out_ref[EDGE:] = target_rows[...].astype(F32).astype(BF)
-
-
-def prepare_kernel(kernels_ref, mask_ref, forward_ref, tap_ref, hat_ref, spectra_ref, slope_ref, stack_ref):
-    stack_ref[...] = jnp.zeros_like(stack_ref)
-    for group in range(NFOC * NK // 4):
-        slot = group % 2
-        for q in range(4):
-            taps = kernels_ref[group * 4 + q]
-            re = taps[:, :NF]
-            im = taps[:, NF:]
-            base = q * 64
-            stack_ref[slot, base : base + TAPS, :NF] = re
-            stack_ref[slot, base : base + TAPS, LANES : LANES + NF] = im
-            stack_ref[slot, base + 32 : base + 32 + TAPS, :NF] = -im
-            stack_ref[slot, base + 32 : base + 32 + TAPS, LANES : LANES + NF] = re
-        hat = dot(tap_ref[...], stack_ref[slot].astype(BF)).astype(BF)
-        hat_ref[group * 4 : group * 4 + 4] = hat.reshape(4, U, 2 * LANES)
+    for d in range(NDOSE):
+        dose_rows_ref[d : d + 1] = jnp.full((1, ROWS), doses[d])
+
+
+def prepare_kernel(
+    kernels_ref, mask_ref, forward_ref, tap_ref, hat_ref, spectra_ref, slope_ref, taps_ref, share_ref, sem
+):
+    column = pl.multiple_of(lax.axis_index("corner") * ROWS, ROWS)
+    share = jnp.tanh(mask_ref[:, pl.ds(column, ROWS)])
+    share_ref[...] = 1.0 - share * share
+    copy = pltpu.make_async_copy(share_ref, slope_ref, sem)
+    copy.start()
+    lane = lax.broadcasted_iota(jnp.int32, (TAP_ROWS, LANES), 1)
+    taps_ref[:, NFOC * TAPS - 4 :] = jnp.zeros((2, TAP_ROWS - NFOC * TAPS + 4, 2 * NF), F32)
+    for kernel in range(NK):
+        slot = kernel % 2
+        for tap in range(TAPS):
+            taps_ref[slot, tap * NFOC : (tap + 1) * NFOC] = kernels_ref[kernel, tap]
+        taps = taps_ref[slot]
+        re = jnp.where(lane < NF, taps[:, :LANES], 0.0)
+        im = jnp.where(lane < NF, pltpu.roll(taps, NF, 1)[:, :LANES], 0.0)
+        hat = dot(tap_ref[...], turned(jnp.concatenate([re, im], axis=1))).astype(BF)
+        hat_ref[kernel * NFOC : (kernel + 1) * NFOC] = hat.reshape(NFOC, U, 2 * LANES)
     field = jnp.tanh(mask_ref[...])
     spectra_ref[...] = dot(field.astype(BF), forward_ref[...]).astype(BF)
-    column = pl.multiple_of(lax.axis_index("corner") * ROWS, ROWS)
-    share = jnp.tanh(mask_ref[:, pl.ds(column, ROWS)])
-    slope_ref[...] = 1.0 - share * share
+    copy.wait()
 
 
 def image_kernel(
@@ -187,7 +198,9 @@
     forward_ref,
     inverse_ref,
     interp_ref,
-    interp_low_ref,
+    forward_t_ref,
+    inverse_t_ref,
+    interp_t_ref,
     window_ref,
     mix_ref,
     unmix_ref,
@@ -213,7 +226,8 @@
         for pair in range(2):
             stack = []
             for q in range(2):
-                hat = hat_ref[group * 4 + pair * 2 + q].astype(F32)
+                kernel = group * 4 + pair * 2 + q
+                hat = hat_ref[(kernel % NK) * NFOC + kernel // NK].astype(F32)
                 hat_re = hat[:, :LANES]
                 hat_im = hat[:, LANES:]
                 re = (mask_re * hat_re - mask_im * hat_im).astype(BF)
@@ -239,7 +253,7 @@
     coarse_high = coarse.astype(BF)
     coarse_low = (coarse - coarse_high.astype(F32)).astype(BF)
     both = dot(jnp.concatenate([coarse_high, coarse_low], axis=0), interp_ref[...])
-    aerial_ref[...] = both[: NFOC * 24] + both[NFOC * 24 :] + dot(coarse_high, interp_low_ref[...])
+    aerial_ref[...] = both[: NFOC * 24] + both[NFOC * 24 :]
     wanted_rows = jnp.concatenate([edge_ref[EDGE:], target_ref[...].astype(F32).astype(BF)], axis=0)
     pick = picked(24, ROWS + TEDGE, SHARE * corner + (TEDGE - RIM))
     band_ref[...] = dot(pick, wanted_rows)
@@ -247,7 +261,7 @@
     pixel = tile * ROWS + SHARE * corner - RIM + local
     valid = (local < SHARE) & (pixel >= 0) & (pixel < ROWS * lax.axis_size("tile"))
     valid = jnp.where(valid, 1.0, 0.0)
-    doses = [dose_ref[d] for d in range(NDOSE)]
+    doses = [dose_ref[d : d + 1] for d in range(NDOSE)]
     for chunk in range(W // ROWS):
         cols = slice(chunk * ROWS, (chunk + 1) * ROWS)
         high = None
@@ -256,13 +270,13 @@
         for focus in range(NFOC):
             aerial = aerial_ref[focus * 24 : (focus + 1) * 24, cols]
             for d in range(NDOSE):
-                level = (0.5 * STEEPNESS * doses[d]) * aerial - 0.5 * STEEPNESS * THRESHOLD
-                resist = 0.5 * jnp.tanh(level) + 0.5
-                up = jnp.exp(SHARPNESS * resist)
-                down = jnp.exp(-SHARPNESS * resist)
+                swing = jnp.tanh((0.5 * STEEPNESS * doses[d]) * aerial - 0.5 * STEEPNESS * THRESHOLD)
+                power = (0.5 * SHARPNESS / math.log(2.0)) * swing + 0.5 * SHARPNESS / math.log(2.0)
+                up = jnp.exp2(power)
+                down = jnp.exp2(-power)
                 high = up if high is None else high + up
                 low_sum = down if low_sum is None else low_sum + down
-                kept.append((resist, up, down))
+                kept.append((swing, up, down))
         wanted = band_ref[:, cols]
         top = jnp.log(high) / SHARPNESS
         bottom = -jnp.log(low_sum) / SHARPNESS
@@ -272,12 +286,12 @@
         for focus in range(NFOC):
             total = None
             for d in range(NDOSE):
-                resist, up, down = kept[focus * NDOSE + d]
-                term = (high_weight * up + low_weight * down) * (resist * (1.0 - resist))
-                term = term * (2.0 * STEEPNESS * doses[d])
+                swing, up, down = kept[focus * NDOSE + d]
+                term = (high_weight * up + low_weight * down) * (1.0 - swing * swing)
+                term = term * (0.5 * STEEPNESS * doses[d])
                 total = term if total is None else total + term
             grad_ref[focus * 24 : (focus + 1) * 24, cols] = total
-    coarse_grad = dot_nt(grad_ref[...].astype(BF), interp_ref[...])
+    coarse_grad = dot(grad_ref[...].astype(BF), interp_t_ref[...])
     acc_re = jnp.zeros((U, LANES), F32)
     acc_im = jnp.zeros((U, LANES), F32)
     for focus in range(NFOC):
@@ -286,23 +300,25 @@
         fold_ref[focus, PAIR : PAIR + 24] = part
         twice = fold_ref[focus, : 2 * PAIR]
         twice = jnp.concatenate([twice, twice], axis=1)
-        twice = jnp.concatenate([twice, twice], axis=0)
+        start = focus * per_focus
+        field_grad = [
+            (twice * field_ref[start + pair * 2 * PAIR : start + (pair + 1) * 2 * PAIR])
+            for pair in range(NK // 2)
+        ]
+        mixed_grad = dot(jnp.concatenate(field_grad, axis=0).astype(BF), inverse_t_ref[...])
         for group in range(NK // 4):
-            start = focus * per_focus + group * 4 * PAIR
-            field_grad = (twice * field_ref[start : start + 4 * PAIR]).astype(BF)
-            mixed_grad = dot_nt(field_grad, inverse_ref[...])
-            hats = dot(unmix_ref[...], turned(mixed_grad))
+            hats = dot(unmix_ref[...], turned(mixed_grad[group * 4 * PAIR : (group + 1) * 4 * PAIR]))
             for q in range(4):
                 grad_re = hats[q * U : (q + 1) * U, :LANES]
                 grad_im = hats[q * U : (q + 1) * U, LANES:]
-                hat = hat_ref[focus * NK + group * 4 + q].astype(F32)
+                hat = hat_ref[(group * 4 + q) * NFOC + focus].astype(F32)
                 hat_re = hat[:, :LANES]
                 hat_im = hat[:, LANES:]
                 acc_re = acc_re + (grad_re * hat_re + grad_im * hat_im)
                 acc_im = acc_im + (grad_im * hat_re - grad_re * hat_im)
     acc = jnp.concatenate([acc_re, acc_im], axis=1) * (1.0 / (TURN * TURN * TURN * U))
     spectra_grad = dot(back_ref[...], turned(acc))
-    mask_grad = dot_nt(spectra_grad.astype(BF), forward_ref[...]).astype(BF)
+    mask_grad = dot(spectra_grad.astype(BF), forward_t_ref[...]).astype(BF)
     for block in range(W // ROWS):
         cols = slice(block * ROWS, (block + 1) * ROWS)
         out_ref[block, :U] = mask_grad[:, cols]
@@ -310,15 +326,12 @@
         out_ref[block, U:] = band.astype(BF)
 
 
-def finish_kernel(blocks_ref, slope_ref, band_ref, grad_ref, sum_ref, rows_ref):
-    sum_ref[...] = jnp.zeros_like(sum_ref)
-    for source in range(blocks_ref.shape[0]):
-        block = blocks_ref[source].astype(F32)
-        start = SHARE * source
-        sum_ref[start : start + U] = sum_ref[start : start + U] + block[:U]
-        rows_ref[start : start + 24] = block[U : U + 24]
-    grad_ref[...] = sum_ref[2 * RIM : 2 * RIM + ROWS] * slope_ref[...]
-    band_ref[...] = rows_ref[RIM : RIM + ROWS]
+def finish_kernel(blocks_ref, slope_ref, place_grad_ref, place_band_ref, band_ref, grad_ref):
+    count = blocks_ref.shape[0]
+    grads = blocks_ref[:, :U].reshape(count * U, ROWS)
+    grad_ref[...] = dot(place_grad_ref[...], grads) * slope_ref[...]
+    bands = blocks_ref[:, U:].reshape(count * (MSG - U), ROWS)
+    band_ref[...] = dot(place_band_ref[...], bands)
 
 
 def params(mib):
@@ -332,18 +345,24 @@
 def per_device(mask_logits, target, kernels, dose_levels):
     tiles = lax.axis_size("tile")
     corners = lax.axis_size("corner")
-    edge = pl.pallas_call(
+    edge, dose_rows = pl.pallas_call(
         edge_kernel,
         name="edge",
-        out_shape=jax.ShapeDtypeStruct((EDGE + TEDGE, W), BF),
-        in_specs=[pl.BlockSpec(memory_space=pl.ANY)] * 2,
-        out_specs=pl.BlockSpec(memory_space=pltpu.VMEM),
+        out_shape=(
+            jax.ShapeDtypeStruct((EDGE + TEDGE, W), BF),
+            jax.ShapeDtypeStruct((NDOSE, ROWS), F32),
+        ),
+        in_specs=[pl.BlockSpec(memory_space=pl.ANY)] * 3,
+        out_specs=tuple(whole(2)),
         scratch_shapes=[
             pltpu.VMEM((EDGE, W), F32),
             pltpu.VMEM((TEDGE, W), jnp.int32),
-            pltpu.SemaphoreType.DMA((2,)),
+            pltpu.SMEM((NDOSE,), F32),
+            pltpu.SemaphoreType.DMA((3,)),
         ],
-    )(mask_logits, target)
+        compiler_params=params(2),
+        cost_estimate=pl.CostEstimate(flops=2_000_000_000, bytes_accessed=0, transcendentals=0),
+    )(*[pltpu.with_memory_space_constraint(x, pltpu.HBM) for x in (mask_logits, target, dose_levels)])
     pairs = []
     for i in range(tiles - 1):
         for c in range(corners):
@@ -355,7 +374,7 @@
     edge = lax.ppermute(edge, ("tile", "corner"), pairs)
     forward = low(forward_table())
     inverse = low(inverse_table())
-    interp, interp_low = low_parts(interpolation_table())
+    interp = low(interpolation_table())
     count = NFOC * NK
     hats, spectra, slope = pl.pallas_call(
         prepare_kernel,
@@ -366,16 +385,20 @@
             jax.ShapeDtypeStruct((ROWS, ROWS), F32),
         ),
         in_specs=whole(4),
-        out_specs=tuple(whole(3)),
-        scratch_shapes=[pltpu.VMEM((2, 256, 2 * LANES), F32)],
-        compiler_params=params(24),
-        cost_estimate=pl.CostEstimate(flops=2_000_000_000, bytes_accessed=8_000_000, transcendentals=0),
-    )(kernels.reshape(count, TAPS, 2 * NF), mask_logits, forward, low(tap_table()))
+        out_specs=tuple(whole(2)) + (pl.BlockSpec(memory_space=pltpu.HBM),),
+        scratch_shapes=[
+            pltpu.VMEM((2, TAP_ROWS, 2 * NF), F32),
+            pltpu.VMEM((ROWS, ROWS), F32),
+            pltpu.SemaphoreType.DMA,
+        ],
+        compiler_params=params(12),
+        cost_estimate=pl.CostEstimate(flops=1_200_000_000, bytes_accessed=0, transcendentals=0),
+    )(kernels.transpose(1, 2, 0, 3), mask_logits, forward, low(tap_table()))
     blocks = pl.pallas_call(
         image_kernel,
         name="image",
         out_shape=jax.ShapeDtypeStruct((W // ROWS, MSG, ROWS), BF),
-        in_specs=[pl.BlockSpec(memory_space=pltpu.SMEM)] + whole(12),
+        in_specs=whole(15),
         out_specs=pl.BlockSpec(memory_space=pltpu.VMEM),
         scratch_shapes=[
             pltpu.VMEM((count * PAIR, 2 * LANES), BF),
@@ -385,10 +408,10 @@
             pltpu.VMEM((NFOC, U, GRID), F32),
             pltpu.VMEM((24, W), F32),
         ],
-        compiler_params=params(32),
+        compiler_params=params(24),
         cost_estimate=pl.CostEstimate(flops=4_000_000_000, bytes_accessed=8_000_000, transcendentals=0),
     )(
-        dose_levels,
+        dose_rows,
         edge,
         spectra,
         target,
@@ -396,12 +419,15 @@
         forward,
         inverse,
         interp,
-        interp_low,
+        low(forward_table().T),
+        low(inverse_table().T),
+        low(interpolation_table().T),
         low(window_table()),
         low(mix_table()),
         low(unmix_table()),
         low(back_table()),
     )
+    place_grad, place_band = placing_tables(corners)
     blocks = lax.all_to_all(blocks, "corner", 0, 0, tiled=True)
     return pl.pallas_call(
         finish_kernel,
@@ -410,10 +436,10 @@
             jax.ShapeDtypeStruct((ROWS, ROWS), F32),
             jax.ShapeDtypeStruct((ROWS, ROWS), F32),
         ),
-        in_specs=whole(2),
+        in_specs=whole(4),
         out_specs=tuple(whole(2)),
-        scratch_shapes=[pltpu.VMEM((192, ROWS), F32), pltpu.VMEM((160, ROWS), F32)],
-    )(blocks, slope)
+        compiler_params=params(4),
+    )(blocks, slope, low(place_grad), low(place_band))
 
 
 def solution(mesh):

time: 40.9 us -> 33.8 us (0.83)
  Pallas kernels: 15.7 us -> 10.1 us
  waiting for transfers between devices: 3.46 us -> 6.24 us
  local copies, waits for them, and re-layouts: 2.52 us -> 0.1 us
  blocking collectives: 16.2 us -> 14.2 us
    pallas_call x1, Pallas kernels: 10.8 us -> 6.84 us  [per_device(): pl.pallas_call(image_kernel, name='image', out_shape=jax.ShapeDtypeStruct...]
    ppermute x1, waiting for transfers between devices: 3.46 us -> 6.24 us  [per_device(): edge = lax.ppermute(edge, ('tile', 'corner'), pairs)]
    unnamed x27 -> x32, local copies, waits for them, and re-layouts: 2.52 us -> 0.1 us
    all_to_all x1, blocking collectives: 16.2 us -> 14.2 us  [per_device(): blocks = lax.all_to_all(blocks, 'corner', 0, 0, tiled=True)]
    pallas_call x1, Pallas kernels: 1.6 us -> 0.83 us  [per_device(): pl.pallas_call(finish_kernel, name='finish', out_shape=(jax.ShapeDtypeStr...]
    pallas_call x1, Pallas kernels: 1.59 us -> 1.13 us  [per_device(): pl.pallas_call(edge_kernel, name='edge', out_shape=(jax.ShapeDtypeStruct(...]
    pallas_call x1, Pallas kernels: 1.69 us -> 1.25 us  [per_device(): pl.pallas_call(prepare_kernel, name='prepare', out_shape=(jax.ShapeDtypeS...]
  transfers between devices with their start and end apart: 1 -> 1, of which waited for: 1 -> 1; matrix products, arithmetic and copies ran while one was open for 4% -> 0% of each run, Pallas kernels for 4% -> 4%
where the time goes in v2:
time: 33.8 us; the launch traced here: 33.6 us
  blocking collectives  14.2 us (42%)
  Pallas kernels  10.1 us (30%)
  waiting for transfers between devices  6.24 us (18%)
  starting transfers between devices  2.18 us (6%)
  between operations  0.88 us (3%)
    all_to_all x1, blocking collectives, per_device(): blocks = lax.all_to_all(blocks, 'corner', 0, 0, tiled=True)  14.2 us
    pallas_call x1, Pallas kernels, per_device(): pl.pallas_call(image_kernel, name='image', out_shape=jax.ShapeDtypeStruct...  6.84 us
    ppermute x1, waiting for transfers between devices, per_device(): edge = lax.ppermute(edge, ('tile', 'corner'), pairs)  6.24 us
    ppermute x1, starting transfers between devices, per_device(): edge = lax.ppermute(edge, ('tile', 'corner'), pairs)  2.18 us
    pallas_call x1, Pallas kernels, per_device(): pl.pallas_call(prepare_kernel, name='prepare', out_shape=(jax.ShapeDtypeS...  1.25 us
    pallas_call x1, Pallas kernels, per_device(): pl.pallas_call(edge_kernel, name='edge', out_shape=(jax.ShapeDtypeStruct(...  1.13 us
    pallas_call x1, Pallas kernels, per_device(): pl.pallas_call(finish_kernel, name='finish', out_shape=(jax.ShapeDtypeStr...  0.83 us
  transfers between devices with their start and end apart: 1, of which 1 were waited for; matrix products, arithmetic and copies ran while one was open for 0% of the time, Pallas kernels for 4%

profile of v2, /device:TPU:2, one launch (start us, length us, event | category | flops | bytes accessed | tf_op | source)
XLA Modules:
  0.0 33.6 jit_solution(17399042513866972407)
XLA Ops:
  0.6 0.0 copy-start.5
  0.6 0.0 copy-start.12
  0.7 0.0 copy-start.3
  0.7 0.0 copy-start.2
  0.7 0.0 copy-start.10
  0.7 1.1 %edge.1 = (bf16[48,1024]{1,0:T(8,128)(2,1)S(1)}, f32[4,128]{1,0:T(4,128)S(1)}) custom-call(f32[128,1024]{1,0:T(8,128)} %mask_ref.3, s32[128,1024]{1,0:T(8,128)} %target_ref.3, f32[4]{0:T(128)} %dose_ref.1), custom_call_target="tpu_custom_call" | custom-call | flops 2000000000 | tf_op jit(solution)/shard_map/edge/pallas_call | solution.py:348
  1.8 0.0 copy-start.4
  1.8 0.0 copy-start.6
  1.8 0.0 copy-start.7
  1.9 0.0 copy-start.8
  1.9 0.0 copy-start.9
  1.9 0.0 copy-start.11
  1.9 0.0 copy-start.13
  1.9 0.0 copy-start.14
  1.9 0.0 copy-start.15
  1.9 2.2 %collective-permute-start = (bf16[48,1024]{1,0:T(8,128)(2,1)S(1)}, bf16[48,1024]{1,0:T(8,128)(2,1)S(1)}, u32[]{:S(2)}, u32[]{:S(2)}) collective-permute-start(bf16[48,1024]{1,0:T(8,128)(2,1)S(1)} %get-tuple-element.8), channel_id=1, source_target_pairs={{0,8},{1,9},{14,6},{15,7},{8,16},{9,17},{22,14},{23,15},{16,24},{1... | collective-permute-start | bytes 294920 | tf_op jit(solution)/shard_map/ppermute | solution.py:374
  4.1 0.0 copy-done.5
  4.1 0.0 copy-done.12
  4.1 0.0 copy-done.3
  4.2 0.0 copy-done.2
  4.2 1.3 %prepare.1 = (bf16[48,48,512]{2,1,0:T(8,128)(2,1)S(1)}, bf16[128,512]{1,0:T(8,128)(2,1)S(1)}, f32[128,128]{1,0:T(8,128)S(1)}) custom-call(f32[12,25,4,384]{3,2,1,0:T(4,128)S(1)} %bitcast.1, f32[128,1024]{1,0:T(8,128)S(1)} %copy-done.3, bf16[1024,512]{1,0:T(8,128)(2,1)S(1)} %copy-done.5, bf16[192,224]{1,0:T(8,128)(2,1)S(1)} %copy-done.12), custom_call_target="tpu_custom_call" | custom-call | flops 1200000000 | tf_op jit(solution)/shard_map/prepare/pallas_call | solution.py:379
  5.4 6.2 %collective-permute-done.edge_ref = bf16[48,1024]{1,0:T(8,128)(2,1)S(1)} collective-permute-done((bf16[48,1024]{1,0:T(8,128)(2,1)S(1)}, bf16[48,1024]{1,0:T(8,128)(2,1)S(1)}, u32[]{:S(2)}, u32[]{:S(2)}) %collective-permute-start) | collective-permute-done | bytes 98336 | tf_op jit(solution)/shard_map/ppermute | solution.py:374
  11.7 0.0 copy-done.10
  11.7 0.0 copy-done.4
  11.7 0.0 copy-done.6
  11.7 0.0 copy-done.7
  11.7 0.0 copy-done.8
  11.7 0.0 copy-done.9
  11.7 0.0 copy-done.11
  11.7 0.0 copy-done.13
  11.7 0.0 copy-done.14
  11.7 0.0 copy-done.15
  11.7 0.0 copy-start
  11.8 0.0 copy-start.1
  11.8 6.8 %image.1 = bf16[8,80,128]{2,1,0:T(8,128)(2,1)S(1)} custom-call(f32[4,128]{1,0:T(4,128)S(1)} %get-tuple-element.7.dose_ref, bf16[48,1024]{1,0:T(8,128)(2,1)S(1)} %collective-permute-done.edge_ref, bf16[128,512]{1,0:T(8,128)(2,1)S(1)} %get-tuple-element.9.spectra_ref, s32[128,1024]{1,0:T(8,128)S(1)} %copy-done.4, ...), custom_call_target="tpu_custom_call" | custom-call | flops 4000000000 | bytes 8000000 | tf_op jit(solution)/shard_map/image/pallas_call | solution.py:397
  18.6 14.2 %all_to_all.5.blocks_ref = bf16[8,80,128]{2,1,0:T(8,128)(2,1)S(1)} all-to-all(bf16[8,80,128]{2,1,0:T(8,128)(2,1)S(1)} %image.1), channel_id=1, replica_groups=mesh['tile'=32,'corner'=8] {'corner'}, dimensions={0} | all-to-all | bytes 327680 | tf_op jit(solution)/shard_map/all_to_all | solution.py:431
  32.8 0.0 copy-done
  32.8 0.0 copy-done.1
  32.8 0.8 %finish.1 = (f32[128,128]{1,0:T(8,128)}, f32[128,128]{1,0:T(8,128)}) custom-call(bf16[8,80,128]{2,1,0:T(8,128)(2,1)S(1)} %all_to_all.5.blocks_ref, f32[128,128]{1,0:T(8,128)S(1)} %get-tuple-element.11.slope_ref, bf16[128,384]{1,0:T(8,128)(2,1)S(1)} %copy-done, bf16[128,256]{1,0:T(8,128)(2,1)S(1)} %copy-done.1), custom_call_target="tpu_custom_call" | custom-call | tf_op jit(solution)/shard_map/finish/pallas_call | solution.py:432
Async XLA Ops:
  0.6 3.5 %copy-start.5 = (bf16[1024,512]{1,0:T(8,128)(2,1)S(1)}, bf16[1024,512]{1,0:T(8,128)(2,1)}, u32[]{:S(2)}) copy-start(bf16[1024,512]{1,0:T(8,128)(2,1)} %constant.39.forward_ref) | copy-start | bytes 3145732
  0.6 3.5 %copy-start.12 = (bf16[192,224]{1,0:T(8,128)(2,1)S(1)}, bf16[192,224]{1,0:T(8,128)(2,1)}, u32[]{:S(2)}) copy-start(bf16[192,224]{1,0:T(8,128)(2,1)} %constant.40.tap_ref) | copy-start | bytes 258052
  0.7 3.5 %copy-start.3 = (f32[128,1024]{1,0:T(8,128)S(1)}, f32[128,1024]{1,0:T(8,128)}, u32[]{:S(2)}) copy-start(f32[128,1024]{1,0:T(8,128)} %mask_ref.3) | copy-start | bytes 1572868
  0.7 3.5 %copy-start.2 = (f32[4,12,25,384]{3,0,2,1:T(4,128)S(1)}, f32[4,12,25,384]{3,0,2,1:T(4,128)}, u32[]{:S(2)}) copy-start(f32[4,12,25,384]{3,0,2,1:T(4,128)} %param.19) | copy-start | bytes 5529604
  0.7 11.0 %copy-start.10 = (bf16[512,768]{1,0:T(8,128)(2,1)S(1)}, bf16[512,768]{1,0:T(8,128)(2,1)}, u32[]{:S(2)}) copy-start(bf16[512,768]{1,0:T(8,128)(2,1)} %constant.41.inverse_ref) | copy-start | bytes 2359300
  1.8 9.9 %copy-start.4 = (s32[128,1024]{1,0:T(8,128)S(1)}, s32[128,1024]{1,0:T(8,128)}, u32[]{:S(2)}) copy-start(s32[128,1024]{1,0:T(8,128)} %target_ref.3) | copy-start | bytes 1572868
  1.8 9.8 %copy-start.6 = (bf16[512,1024]{1,0:T(8,128)(2,1)S(1)}, bf16[512,1024]{1,0:T(8,128)(2,1)}, u32[]{:S(2)}) copy-start(bf16[512,1024]{1,0:T(8,128)(2,1)} %constant.43.forward_t_ref) | copy-start | bytes 3145732
  1.8 9.8 %copy-start.7 = (bf16[1024,384]{1,0:T(8,128)(2,1)S(1)}, bf16[1024,384]{1,0:T(8,128)(2,1)}, u32[]{:S(2)}) copy-start(bf16[1024,384]{1,0:T(8,128)(2,1)} %constant.45.interp_t_ref) | copy-start | bytes 2359300
  1.9 9.8 %copy-start.8 = (bf16[768,512]{1,0:T(8,128)(2,1)S(1)}, bf16[768,512]{1,0:T(8,128)(2,1)}, u32[]{:S(2)}) copy-start(bf16[768,512]{1,0:T(8,128)(2,1)} %constant.44.inverse_t_ref) | copy-start | bytes 2359300
  1.9 9.8 %copy-start.9 = (bf16[384,1024]{1,0:T(8,128)(2,1)S(1)}, bf16[384,1024]{1,0:T(8,128)(2,1)}, u32[]{:S(2)}) copy-start(bf16[384,1024]{1,0:T(8,128)(2,1)} %constant.42.interp_ref) | copy-start | bytes 2359300
  1.9 9.8 %copy-start.11 = (bf16[192,160]{1,0:T(8,128)(2,1)S(1)}, bf16[192,160]{1,0:T(8,128)(2,1)}, u32[]{:S(2)}) copy-start(bf16[192,160]{1,0:T(8,128)(2,1)} %constant.48.unmix_ref) | copy-start | bytes 184324
  1.9 9.8 %copy-start.13 = (bf16[40,192]{1,0:T(8,128)(2,1)S(1)}, bf16[40,192]{1,0:T(8,128)(2,1)}, u32[]{:S(2)}) copy-start(bf16[40,192]{1,0:T(8,128)(2,1)} %constant.47.mix_ref) | copy-start | bytes 46084
  1.9 9.8 %copy-start.14 = (bf16[48,96]{1,0:T(8,128)(2,1)S(1)}, bf16[48,96]{1,0:T(8,128)(2,1)}, u32[]{:S(2)}) copy-start(bf16[48,96]{1,0:T(8,128)(2,1)} %constant.49.back_ref) | copy-start | bytes 27652
  1.9 9.8 %copy-start.15 = (bf16[48,96]{1,0:T(8,128)(2,1)S(1)}, bf16[48,96]{1,0:T(8,128)(2,1)}, u32[]{:S(2)}) copy-start(bf16[48,96]{1,0:T(8,128)(2,1)} %constant.46.window_ref) | copy-start | bytes 27652
  1.9 9.7 %collective-permute-start = (bf16[48,1024]{1,0:T(8,128)(2,1)S(1)}, bf16[48,1024]{1,0:T(8,128)(2,1)S(1)}, u32[]{:S(2)}, u32[]{:S(2)}) collective-permute-start(bf16[48,1024]{1,0:T(8,128)(2,1)S(1)} %get-tuple-element.8), channel_id=1, source_target_pairs={{0,8},{1,9},{14,6},{15,7},{8,16},{9,17},{22,14},{23,15},{16,24},{1... | collective-permute-start | bytes 294920 | tf_op jit(solution)/shard_map/ppermute | solution.py:374
  11.7 21.1 %copy-start = (bf16[128,384]{1,0:T(8,128)(2,1)S(1)}, bf16[128,384]{1,0:T(8,128)(2,1)}, u32[]{:S(2)}) copy-start(bf16[128,384]{1,0:T(8,128)(2,1)} %constant.50.place_grad_ref) | copy-start | bytes 294916
  11.8 21.0 %copy-start.1 = (bf16[128,256]{1,0:T(8,128)(2,1)S(1)}, bf16[128,256]{1,0:T(8,128)(2,1)}, u32[]{:S(2)}) copy-start(bf16[128,256]{1,0:T(8,128)(2,1)} %constant.51.place_band_ref) | copy-start | bytes 196612

commit v3 on v2

--- a/solution.py
+++ b/solution.py
@@ -32,6 +32,7 @@
 EDGE = 32
 TEDGE = 16
 MSG = 48 + 32
+WINDOW = (0, 1, 7, 2, 6, 3, 4, 5)
 TURN = 1.62425
 
 
@@ -74,18 +75,20 @@
     return 2.0 * math.pi * (np.outer(np.arange(left), np.arange(right)) % U) / U
 
 
+def complex_table(angle):
+    return TURN * np.block([[np.cos(angle), -np.sin(angle)], [np.sin(angle), np.cos(angle)]])
+
+
 def tap_table():
-    angle = row_angles(U, TAPS)
-    table = np.zeros((NFOC, U, 2, TAP_ROWS))
+    table = complex_table(row_angles(U, TAPS)).reshape(2, U, 2, TAPS)
+    full = np.zeros((NFOC, 2, U, 2, TAP_ROWS))
     for focus in range(NFOC):
-        table[focus, :, 0, focus : TAPS * NFOC : NFOC] = np.cos(angle)
-        table[focus, :, 1, focus : TAPS * NFOC : NFOC] = np.sin(angle)
-    return TURN * table.reshape(NFOC * U, 2 * TAP_ROWS)
+        full[focus, :, :, :, focus : TAPS * NFOC : NFOC] = table
+    return full.reshape(NFOC * 2 * U, 2 * TAP_ROWS)
 
 
 def window_table():
-    angle = row_angles(U, U)
-    return TURN * np.concatenate([np.cos(angle), -np.sin(angle)], axis=1)
+    return complex_table(-row_angles(U, U))
 
 
 def back_table():
@@ -94,24 +97,42 @@
 
 
 def mix_table(count=2):
-    angle = row_angles(PAIR, U)
-    table = np.zeros((count * PAIR, count * 2 * U))
+    table = complex_table(row_angles(PAIR, U)).reshape(2, PAIR, 2, U)
+    full = np.zeros((2, count, PAIR, count, 2, U))
     for q in range(count):
-        rows = slice(q * PAIR, (q + 1) * PAIR)
-        table[rows, q * 2 * U : q * 2 * U + U] = np.cos(angle)
-        table[rows, q * 2 * U + U : (q + 1) * 2 * U] = np.sin(angle)
-    return TURN * table
-
-
-def unmix_table(count=4):
-    angle = row_angles(U, PAIR)
-    half = count * PAIR
-    table = np.zeros((count * U, 2 * half))
+        full[:, q, :, q] = table
+    return full.reshape(2 * count * PAIR, count * 2 * U)
+
+
+def unmix_table(count=6):
+    table = complex_table(-row_angles(U, PAIR)).reshape(2, U, 2, PAIR)
+    full = np.zeros((count, 2, U, 2, count, PAIR))
     for q in range(count):
-        rows = slice(q * U, (q + 1) * U)
-        table[rows, q * PAIR : (q + 1) * PAIR] = np.cos(angle)
-        table[rows, half + q * PAIR : half + (q + 1) * PAIR] = -np.sin(angle)
-    return TURN * table
+        full[q, :, :, :, q] = table
+    return full.reshape(count * 2 * U, 2 * count * PAIR)
+
+
+def entry_table():
+    taps = tap_table()
+    half = taps.shape[0] // 2
+    table = np.zeros((W + half, 2 * LANES))
+    table[:W] = forward_table()
+    table[W:, : taps.shape[1]] = taps[:half]
+    table[W:, LANES : LANES + taps.shape[1]] = taps[half:]
+    return table
+
+
+def row_tables():
+    tables = [window_table(), mix_table(), unmix_table(), back_table()]
+    places = []
+    first = 0
+    for table in tables:
+        places.append((slice(first, first + table.shape[0]), slice(0, table.shape[1])))
+        first += table.shape[0]
+    whole_table = np.zeros((first, LANES))
+    for table, place in zip(tables, places):
+        whole_table[place] = table
+    return whole_table, places
 
 
 def placing_tables(count):
@@ -119,11 +140,11 @@
     band = np.zeros((ROWS, count, MSG - U))
     for source in range(count):
         for row in range(SHARE + 2 * RIM):
-            pixel = SHARE * source + row - 2 * RIM
+            pixel = SHARE * WINDOW[source] + row - 2 * RIM
             if 0 <= pixel < ROWS:
                 grad[pixel, source, row] = 1.0
         for row in range(SHARE):
-            pixel = SHARE * source + row - RIM
+            pixel = SHARE * WINDOW[source] + row - RIM
             if 0 <= pixel < ROWS:
                 band[pixel, source, row] = 1.0
     return grad.reshape(ROWS, -1), band.reshape(ROWS, -1)
@@ -133,10 +154,16 @@
     return jnp.dot(left, right, preferred_element_type=F32)
 
 
-def turned(value):
-    value = value.astype(BF)
-    swapped = jnp.concatenate([-value[:, LANES:], value[:, :LANES]], axis=1)
-    return jnp.concatenate([value, swapped], axis=0)
+def window_here():
+    corner = lax.axis_index("corner")
+    window = jnp.int32(WINDOW[0])
+    for n in range(1, len(WINDOW)):
+        window = jnp.where(corner == n, WINDOW[n], window)
+    return window
+
+
+def stacked(value):
+    return jnp.concatenate([value[:, :LANES], value[:, LANES:]], axis=0).astype(BF)
 
 
 def picked(count, length, first):
@@ -147,7 +174,7 @@
 
 
 def edge_kernel(mask_ref, target_ref, dose_ref, out_ref, dose_rows_ref, mask_rows, target_rows, doses, sems):
-    down = lax.axis_index("corner") < lax.axis_size("corner") // 2
+    down = window_here() < len(WINDOW) // 2
     mask_from = pl.multiple_of(jnp.where(down, ROWS - EDGE, 0), EDGE)
     target_from = pl.multiple_of(jnp.where(down, ROWS - TEDGE, 0), TEDGE)
     copies = [
@@ -166,7 +193,7 @@
 
 
 def prepare_kernel(
-    kernels_ref, mask_ref, forward_ref, tap_ref, hat_ref, spectra_ref, slope_ref, taps_ref, share_ref, sem
+    kernels_ref, mask_ref, entry_ref, hat_ref, spectra_ref, slope_ref, taps_ref, share_ref, sem
 ):
     column = pl.multiple_of(lax.axis_index("corner") * ROWS, ROWS)
     share = jnp.tanh(mask_ref[:, pl.ds(column, ROWS)])
@@ -174,18 +201,31 @@
     copy = pltpu.make_async_copy(share_ref, slope_ref, sem)
     copy.start()
     lane = lax.broadcasted_iota(jnp.int32, (TAP_ROWS, LANES), 1)
-    taps_ref[:, NFOC * TAPS - 4 :] = jnp.zeros((2, TAP_ROWS - NFOC * TAPS + 4, 2 * NF), F32)
-    for kernel in range(NK):
-        slot = kernel % 2
-        for tap in range(TAPS):
-            taps_ref[slot, tap * NFOC : (tap + 1) * NFOC] = kernels_ref[kernel, tap]
-        taps = taps_ref[slot]
-        re = jnp.where(lane < NF, taps[:, :LANES], 0.0)
-        im = jnp.where(lane < NF, pltpu.roll(taps, NF, 1)[:, :LANES], 0.0)
-        hat = dot(tap_ref[...], turned(jnp.concatenate([re, im], axis=1))).astype(BF)
-        hat_ref[kernel * NFOC : (kernel + 1) * NFOC] = hat.reshape(NFOC, U, 2 * LANES)
+    taps_ref[:, :, NFOC * TAPS - 4 :] = jnp.zeros((2, 2, TAP_ROWS - NFOC * TAPS + 4, 2 * NF), F32)
+    half = NFOC * U
+    table = jnp.concatenate(
+        [
+            entry_ref[W : W + half, : 2 * TAP_ROWS],
+            entry_ref[W : W + half, LANES : LANES + 2 * TAP_ROWS],
+        ],
+        axis=0,
+    )
+    for kernel in range(0, NK, 2):
+        slot = kernel // 2 % 2
+        parts = []
+        for q in range(2):
+            for tap in range(TAPS):
+                taps_ref[slot, q, tap * NFOC : (tap + 1) * NFOC] = kernels_ref[kernel + q, tap]
+            taps = taps_ref[slot, q]
+            re = jnp.where(lane < NF, taps[:, :LANES], 0.0)
+            im = jnp.where(lane < NF, pltpu.roll(taps, NF, 1)[:, :LANES], 0.0)
+            parts.append(jnp.concatenate([re, im], axis=0).astype(BF))
+        hats = dot(table, jnp.concatenate(parts, axis=1))
+        for q in range(2):
+            hat = hats[:, q * LANES : (q + 1) * LANES].reshape(NFOC, 2 * U, LANES)
+            hat_ref[(kernel + q) * NFOC : (kernel + q + 1) * NFOC] = hat
     field = jnp.tanh(mask_ref[...])
-    spectra_ref[...] = dot(field.astype(BF), forward_ref[...]).astype(BF)
+    spectra_ref[...] = dot(field.astype(BF), entry_ref[:W]).astype(BF)
     copy.wait()
 
 
@@ -195,16 +235,13 @@
     spectra_ref,
     target_ref,
     hat_ref,
-    forward_ref,
+    entry_ref,
     inverse_ref,
     interp_ref,
     forward_t_ref,
     inverse_t_ref,
     interp_t_ref,
-    window_ref,
-    mix_ref,
-    unmix_ref,
-    back_ref,
+    rows_ref,
     out_ref,
     mixed_ref,
     field_ref,
@@ -213,28 +250,30 @@
     fold_ref,
     band_ref,
 ):
-    corner = lax.axis_index("corner")
+    window = window_here()
     tile = lax.axis_index("tile")
-    edge = dot(edge_ref[:EDGE], forward_ref[...]).astype(BF)
+    window_rows, mix_rows, unmix_rows, back_rows = row_tables()[1]
+    edge = dot(edge_ref[:EDGE], entry_ref[:W]).astype(BF)
     rows = jnp.concatenate([edge, spectra_ref[...]], axis=0)
-    pick = picked(U, ROWS + EDGE, SHARE * corner + (EDGE - 2 * RIM))
-    mask_hat = dot(window_ref[...], turned(dot(pick, rows))) * (1.0 / (TURN * TURN * TURN * U))
-    mask_re = mask_hat[:, :LANES]
-    mask_im = mask_hat[:, LANES:]
+    pick = picked(U, ROWS + EDGE, SHARE * window + (EDGE - 2 * RIM))
+    mask_hat = dot(rows_ref[window_rows], stacked(dot(pick, rows))) * (1.0 / (TURN * TURN * TURN * U))
+    mask_re = mask_hat[:U]
+    mask_im = mask_hat[U:]
     for group in range(NFOC * NK // 4):
-        parts = []
+        stacks = []
         for pair in range(2):
             stack = []
             for q in range(2):
                 kernel = group * 4 + pair * 2 + q
-                hat = hat_ref[(kernel % NK) * NFOC + kernel // NK].astype(F32)
-                hat_re = hat[:, :LANES]
-                hat_im = hat[:, LANES:]
-                re = (mask_re * hat_re - mask_im * hat_im).astype(BF)
-                im = (mask_re * hat_im + mask_im * hat_re).astype(BF)
-                stack.append(jnp.concatenate([re, im], axis=1))
-                stack.append(jnp.concatenate([-im, re], axis=1))
-            parts.append(dot(mix_ref[...], jnp.concatenate(stack, axis=0)))
+                hat = hat_ref[(kernel % NK) * NFOC + kernel // NK]
+                stack.append(mask_re * hat[:U] - mask_im * hat[U:])
+                stack.append(mask_re * hat[U:] + mask_im * hat[:U])
+            stacks.append(jnp.concatenate(stack, axis=0).astype(BF))
+        mixed = dot(rows_ref[mix_rows], jnp.concatenate(stacks, axis=1))
+        parts = []
+        for pair in range(2):
+            lanes = slice(pair * LANES, (pair + 1) * LANES)
+            parts.append(jnp.concatenate([mixed[: 2 * PAIR, lanes], mixed[2 * PAIR :, lanes]], axis=1))
         mixed_ref[group * 4 * PAIR : (group + 1) * 4 * PAIR] = jnp.concatenate(parts, axis=0).astype(BF)
     per_focus = NK * PAIR
     fold_ref[...] = jnp.zeros_like(fold_ref)
@@ -255,10 +294,10 @@
     both = dot(jnp.concatenate([coarse_high, coarse_low], axis=0), interp_ref[...])
     aerial_ref[...] = both[: NFOC * 24] + both[NFOC * 24 :]
     wanted_rows = jnp.concatenate([edge_ref[EDGE:], target_ref[...].astype(F32).astype(BF)], axis=0)
-    pick = picked(24, ROWS + TEDGE, SHARE * corner + (TEDGE - RIM))
+    pick = picked(24, ROWS + TEDGE, SHARE * window + (TEDGE - RIM))
     band_ref[...] = dot(pick, wanted_rows)
     local = lax.broadcasted_iota(jnp.int32, (24, ROWS), 0)
-    pixel = tile * ROWS + SHARE * corner - RIM + local
+    pixel = tile * ROWS + SHARE * window - RIM + local
     valid = (local < SHARE) & (pixel >= 0) & (pixel < ROWS * lax.axis_size("tile"))
     valid = jnp.where(valid, 1.0, 0.0)
     doses = [dose_ref[d : d + 1] for d in range(NDOSE)]
@@ -306,18 +345,22 @@
             for pair in range(NK // 2)
         ]
         mixed_grad = dot(jnp.concatenate(field_grad, axis=0).astype(BF), inverse_t_ref[...])
-        for group in range(NK // 4):
-            hats = dot(unmix_ref[...], turned(mixed_grad[group * 4 * PAIR : (group + 1) * 4 * PAIR]))
-            for q in range(4):
-                grad_re = hats[q * U : (q + 1) * U, :LANES]
-                grad_im = hats[q * U : (q + 1) * U, LANES:]
-                hat = hat_ref[(group * 4 + q) * NFOC + focus].astype(F32)
-                hat_re = hat[:, :LANES]
-                hat_im = hat[:, LANES:]
-                acc_re = acc_re + (grad_re * hat_re + grad_im * hat_im)
-                acc_im = acc_im + (grad_im * hat_re - grad_re * hat_im)
-    acc = jnp.concatenate([acc_re, acc_im], axis=1) * (1.0 / (TURN * TURN * TURN * U))
-    spectra_grad = dot(back_ref[...], turned(acc))
+        grads = [stacked(mixed_grad[group * 6 * PAIR : (group + 1) * 6 * PAIR]) for group in range(NK // 6)]
+        grads = dot(rows_ref[unmix_rows], jnp.concatenate(grads, axis=1))
+        for group in range(NK // 6):
+            lanes = slice(group * LANES, (group + 1) * LANES)
+            for q in range(6):
+                grad_re = grads[2 * q * U : (2 * q + 1) * U, lanes]
+                grad_im = grads[(2 * q + 1) * U : (2 * q + 2) * U, lanes]
+                hat = hat_ref[(group * 6 + q) * NFOC + focus]
+                acc_re = acc_re + (grad_re * hat[:U] + grad_im * hat[U:])
+                acc_im = acc_im + (grad_im * hat[:U] - grad_re * hat[U:])
+    acc_re = acc_re * (1.0 / (TURN * TURN * TURN * U))
+    acc_im = acc_im * (1.0 / (TURN * TURN * TURN * U))
+    acc = jnp.concatenate(
+        [jnp.concatenate([acc_re, acc_im], axis=1), jnp.concatenate([-acc_im, acc_re], axis=1)], axis=0
+    )
+    spectra_grad = dot(rows_ref[back_rows], acc.astype(BF))
     mask_grad = dot(spectra_grad.astype(BF), forward_t_ref[...]).astype(BF)
     for block in range(W // ROWS):
         cols = slice(block * ROWS, (block + 1) * ROWS)
@@ -366,13 +409,13 @@
     pairs = []
     for i in range(tiles - 1):
         for c in range(corners):
-            begin = SHARE * c - 2 * RIM
+            begin = SHARE * WINDOW[c] - 2 * RIM
             if begin < 0:
                 pairs.append((i * corners + c, (i + 1) * corners + c))
             elif begin + SHARE + 2 * RIM > ROWS:
                 pairs.append(((i + 1) * corners + c, i * corners + c))
     edge = lax.ppermute(edge, ("tile", "corner"), pairs)
-    forward = low(forward_table())
+    entry = low(entry_table())
     inverse = low(inverse_table())
     interp = low(interpolation_table())
     count = NFOC * NK
@@ -380,25 +423,25 @@
         prepare_kernel,
         name="prepare",
         out_shape=(
-            jax.ShapeDtypeStruct((count, U, 2 * LANES), BF),
+            jax.ShapeDtypeStruct((count, 2 * U, LANES), F32),
             jax.ShapeDtypeStruct((ROWS, 2 * LANES), BF),
             jax.ShapeDtypeStruct((ROWS, ROWS), F32),
         ),
-        in_specs=whole(4),
+        in_specs=whole(3),
         out_specs=tuple(whole(2)) + (pl.BlockSpec(memory_space=pltpu.HBM),),
         scratch_shapes=[
-            pltpu.VMEM((2, TAP_ROWS, 2 * NF), F32),
+            pltpu.VMEM((2, 2, TAP_ROWS, 2 * NF), F32),
             pltpu.VMEM((ROWS, ROWS), F32),
             pltpu.SemaphoreType.DMA,
         ],
-        compiler_params=params(12),
+        compiler_params=params(6),
         cost_estimate=pl.CostEstimate(flops=1_200_000_000, bytes_accessed=0, transcendentals=0),
-    )(kernels.transpose(1, 2, 0, 3), mask_logits, forward, low(tap_table()))
+    )(kernels.transpose(1, 2, 0, 3), mask_logits, entry)
     blocks = pl.pallas_call(
         image_kernel,
         name="image",
         out_shape=jax.ShapeDtypeStruct((W // ROWS, MSG, ROWS), BF),
-        in_specs=whole(15),
+        in_specs=whole(12),
         out_specs=pl.BlockSpec(memory_space=pltpu.VMEM),
         scratch_shapes=[
             pltpu.VMEM((count * PAIR, 2 * LANES), BF),
@@ -408,7 +451,7 @@
             pltpu.VMEM((NFOC, U, GRID), F32),
             pltpu.VMEM((24, W), F32),
         ],
-        compiler_params=params(24),
+        compiler_params=params(14),
         cost_estimate=pl.CostEstimate(flops=4_000_000_000, bytes_accessed=8_000_000, transcendentals=0),
     )(
         dose_rows,
@@ -416,16 +459,13 @@
         spectra,
         target,
         hats,
-        forward,
+        entry,
         inverse,
         interp,
         low(forward_table().T),
         low(inverse_table().T),
         low(interpolation_table().T),
-        low(window_table()),
-        low(mix_table()),
-        low(unmix_table()),
-        low(back_table()),
+        low(row_tables()[0]),
     )
     place_grad, place_band = placing_tables(corners)
     blocks = lax.all_to_all(blocks, "corner", 0, 0, tiled=True)

time: 33.8 us -> 31.8 us (0.941)
  blocking collectives: 14.2 us -> 12.5 us
    all_to_all x1, blocking collectives: 14.2 us -> 12.5 us  [per_device(): blocks = lax.all_to_all(blocks, 'corner', 0, 0, tiled=True)]
where the time goes in v3:
time: 31.8 us; the launch traced here: 31.6 us
  blocking collectives  12.5 us (39%)
  Pallas kernels  10.1 us (32%)
  waiting for transfers between devices  6.09 us (19%)
  starting transfers between devices  2.05 us (6%)
  between operations  0.82 us (3%)
    all_to_all x1, blocking collectives, per_device(): blocks = lax.all_to_all(blocks, 'corner', 0, 0, tiled=True)  12.5 us
    pallas_call x1, Pallas kernels, per_device(): pl.pallas_call(image_kernel, name='image', out_shape=jax.ShapeDtypeStruct...  6.8 us
    ppermute x1, waiting for transfers between devices, per_device(): edge = lax.ppermute(edge, ('tile', 'corner'), pairs)  6.09 us
    ppermute x1, starting transfers between devices, per_device(): edge = lax.ppermute(edge, ('tile', 'corner'), pairs)  2.05 us
    pallas_call x1, Pallas kernels, per_device(): pl.pallas_call(prepare_kernel, name='prepare', out_shape=(jax.ShapeDtypeS...  1.34 us
    pallas_call x1, Pallas kernels, per_device(): pl.pallas_call(edge_kernel, name='edge', out_shape=(jax.ShapeDtypeStruct(...  1.13 us
    pallas_call x1, Pallas kernels, per_device(): pl.pallas_call(finish_kernel, name='finish', out_shape=(jax.ShapeDtypeStr...  0.84 us
  transfers between devices with their start and end apart: 1, of which 1 were waited for; matrix products, arithmetic and copies ran while one was open for 0% of the time, Pallas kernels for 4%

profile of v3, /device:TPU:2, one launch (start us, length us, event | category | flops | bytes accessed | tf_op | source)
XLA Modules:
  0.0 31.6 jit_solution(10566541315333604737)
XLA Ops:
  0.6 0.0 copy-start.5
  0.6 0.0 copy-start.3
  0.7 0.0 copy-start.2
  0.7 0.0 copy-start.10
  0.7 1.1 %edge.1 = (bf16[48,1024]{1,0:T(8,128)(2,1)S(1)}, f32[4,128]{1,0:T(4,128)S(1)}) custom-call(f32[128,1024]{1,0:T(8,128)} %mask_ref.3, s32[128,1024]{1,0:T(8,128)} %target_ref.3, f32[4]{0:T(128)} %dose_ref.1), custom_call_target="tpu_custom_call" | custom-call | flops 2000000000 | tf_op jit(solution)/shard_map/edge/pallas_call | solution.py:391
  1.8 2.1 %collective-permute-start = (bf16[48,1024]{1,0:T(8,128)(2,1)S(1)}, bf16[48,1024]{1,0:T(8,128)(2,1)S(1)}, u32[]{:S(2)}, u32[]{:S(2)}) collective-permute-start(bf16[48,1024]{1,0:T(8,128)(2,1)S(1)} %get-tuple-element.8), channel_id=1, source_target_pairs={{0,8},{1,9},{10,2},{12,4},{8,16},{9,17},{18,10},{20,12},{16,24},{1... | collective-permute-start | bytes 294920 | tf_op jit(solution)/shard_map/ppermute | solution.py:417
  3.9 0.0 copy-done.5
  3.9 0.0 copy-done.3
  3.9 0.0 copy-done.2
  3.9 0.0 copy-start.4
  3.9 0.0 copy-start.6
  3.9 0.0 copy-start.7
  3.9 0.0 copy-start.8
  4.0 0.0 copy-start.9
  4.0 0.0 copy-start.11
  4.0 1.3 %prepare.1 = (f32[48,96,256]{2,1,0:T(8,128)S(1)}, bf16[128,512]{1,0:T(8,128)(2,1)S(1)}, f32[128,128]{1,0:T(8,128)S(1)}) custom-call(f32[12,25,4,384]{3,2,1,0:T(4,128)S(1)} %bitcast.1, f32[128,1024]{1,0:T(8,128)S(1)} %copy-done.3, bf16[1216,512]{1,0:T(8,128)(2,1)S(1)} %copy-done.5), custom_call_target="tpu_custom_call" | custom-call | flops 1200000000 | tf_op jit(solution)/shard_map/prepare/pallas_call | solution.py:422
  5.3 6.1 %collective-permute-done.edge_ref = bf16[48,1024]{1,0:T(8,128)(2,1)S(1)} collective-permute-done((bf16[48,1024]{1,0:T(8,128)(2,1)S(1)}, bf16[48,1024]{1,0:T(8,128)(2,1)S(1)}, u32[]{:S(2)}, u32[]{:S(2)}) %collective-permute-start) | collective-permute-done | bytes 98336 | tf_op jit(solution)/shard_map/ppermute | solution.py:417
  11.4 0.0 copy-done.10
  11.4 0.0 copy-done.4
  11.4 0.0 copy-done.6
  11.4 0.0 copy-done.7
  11.4 0.0 copy-done.8
  11.4 0.0 copy-done.9
  11.5 0.0 copy-done.11
  11.5 0.0 copy-start
  11.5 0.0 copy-start.1
  11.5 6.8 %image.1 = bf16[8,80,128]{2,1,0:T(8,128)(2,1)S(1)} custom-call(f32[4,128]{1,0:T(4,128)S(1)} %get-tuple-element.7.dose_ref, bf16[48,1024]{1,0:T(8,128)(2,1)S(1)} %collective-permute-done.edge_ref, bf16[128,512]{1,0:T(8,128)(2,1)S(1)} %get-tuple-element.9.spectra_ref, s32[128,1024]{1,0:T(8,128)S(1)} %copy-done.4, ...), custom_call_target="tpu_custom_call" | custom-call | flops 4000000000 | bytes 8000000 | tf_op jit(solution)/shard_map/image/pallas_call | solution.py:440
  18.3 12.5 %all_to_all.5.blocks_ref = bf16[8,80,128]{2,1,0:T(8,128)(2,1)S(1)} all-to-all(bf16[8,80,128]{2,1,0:T(8,128)(2,1)S(1)} %image.1), channel_id=1, replica_groups=mesh['tile'=32,'corner'=8] {'corner'}, dimensions={0} | all-to-all | bytes 327680 | tf_op jit(solution)/shard_map/all_to_all | solution.py:471
  30.8 0.0 copy-done
  30.8 0.0 copy-done.1
  30.8 0.8 %finish.1 = (f32[128,128]{1,0:T(8,128)}, f32[128,128]{1,0:T(8,128)}) custom-call(bf16[8,80,128]{2,1,0:T(8,128)(2,1)S(1)} %all_to_all.5.blocks_ref, f32[128,128]{1,0:T(8,128)S(1)} %get-tuple-element.11.slope_ref, bf16[128,384]{1,0:T(8,128)(2,1)S(1)} %copy-done, bf16[128,256]{1,0:T(8,128)(2,1)S(1)} %copy-done.1), custom_call_target="tpu_custom_call" | custom-call | tf_op jit(solution)/shard_map/finish/pallas_call | solution.py:472
Async XLA Ops:
  0.6 3.2 %copy-start.5 = (bf16[1216,512]{1,0:T(8,128)(2,1)S(1)}, bf16[1216,512]{1,0:T(8,128)(2,1)}, u32[]{:S(2)}) copy-start(bf16[1216,512]{1,0:T(8,128)(2,1)} %constant.27.entry_ref) | copy-start | bytes 3735556
  0.6 3.2 %copy-start.3 = (f32[128,1024]{1,0:T(8,128)S(1)}, f32[128,1024]{1,0:T(8,128)}, u32[]{:S(2)}) copy-start(f32[128,1024]{1,0:T(8,128)} %mask_ref.3) | copy-start | bytes 1572868
  0.7 3.2 %copy-start.2 = (f32[4,12,25,384]{3,0,2,1:T(4,128)S(1)}, f32[4,12,25,384]{3,0,2,1:T(4,128)}, u32[]{:S(2)}) copy-start(f32[4,12,25,384]{3,0,2,1:T(4,128)} %param.15) | copy-start | bytes 5529604
  0.7 10.8 %copy-start.10 = (bf16[512,768]{1,0:T(8,128)(2,1)S(1)}, bf16[512,768]{1,0:T(8,128)(2,1)}, u32[]{:S(2)}) copy-start(bf16[512,768]{1,0:T(8,128)(2,1)} %constant.28.inverse_ref) | copy-start | bytes 2359300
  1.8 9.6 %collective-permute-start = (bf16[48,1024]{1,0:T(8,128)(2,1)S(1)}, bf16[48,1024]{1,0:T(8,128)(2,1)S(1)}, u32[]{:S(2)}, u32[]{:S(2)}) collective-permute-start(bf16[48,1024]{1,0:T(8,128)(2,1)S(1)} %get-tuple-element.8), channel_id=1, source_target_pairs={{0,8},{1,9},{10,2},{12,4},{8,16},{9,17},{18,10},{20,12},{16,24},{1... | collective-permute-start | bytes 294920 | tf_op jit(solution)/shard_map/ppermute | solution.py:417
  3.9 7.5 %copy-start.4 = (s32[128,1024]{1,0:T(8,128)S(1)}, s32[128,1024]{1,0:T(8,128)}, u32[]{:S(2)}) copy-start(s32[128,1024]{1,0:T(8,128)} %target_ref.3) | copy-start | bytes 1572868
  3.9 7.5 %copy-start.6 = (bf16[512,1024]{1,0:T(8,128)(2,1)S(1)}, bf16[512,1024]{1,0:T(8,128)(2,1)}, u32[]{:S(2)}) copy-start(bf16[512,1024]{1,0:T(8,128)(2,1)} %constant.30.forward_t_ref) | copy-start | bytes 3145732
  3.9 7.5 %copy-start.7 = (bf16[1024,384]{1,0:T(8,128)(2,1)S(1)}, bf16[1024,384]{1,0:T(8,128)(2,1)}, u32[]{:S(2)}) copy-start(bf16[1024,384]{1,0:T(8,128)(2,1)} %constant.32.interp_t_ref) | copy-start | bytes 2359300
  3.9 7.5 %copy-start.8 = (bf16[768,512]{1,0:T(8,128)(2,1)S(1)}, bf16[768,512]{1,0:T(8,128)(2,1)}, u32[]{:S(2)}) copy-start(bf16[768,512]{1,0:T(8,128)(2,1)} %constant.31.inverse_t_ref) | copy-start | bytes 2359300
  4.0 7.5 %copy-start.9 = (bf16[384,1024]{1,0:T(8,128)(2,1)S(1)}, bf16[384,1024]{1,0:T(8,128)(2,1)}, u32[]{:S(2)}) copy-start(bf16[384,1024]{1,0:T(8,128)(2,1)} %constant.29.interp_ref) | copy-start | bytes 2359300
  4.0 7.5 %copy-start.11 = (bf16[800,256]{1,0:T(8,128)(2,1)S(1)}, bf16[800,256]{1,0:T(8,128)(2,1)}, u32[]{:S(2)}) copy-start(bf16[800,256]{1,0:T(8,128)(2,1)} %constant.33.rows_ref) | copy-start | bytes 1228804
  11.5 19.3 %copy-start = (bf16[128,384]{1,0:T(8,128)(2,1)S(1)}, bf16[128,384]{1,0:T(8,128)(2,1)}, u32[]{:S(2)}) copy-start(bf16[128,384]{1,0:T(8,128)(2,1)} %constant.34.place_grad_ref) | copy-start | bytes 294916
  11.5 19.3 %copy-start.1 = (bf16[128,256]{1,0:T(8,128)(2,1)S(1)}, bf16[128,256]{1,0:T(8,128)(2,1)}, u32[]{:S(2)}) copy-start(bf16[128,256]{1,0:T(8,128)(2,1)} %constant.35.place_band_ref) | copy-start | bytes 196612

commit v4 on v3

v4 whole, which is shorter than its diff:
```python
import math

import jax
import jax.numpy as jnp
import numpy as np
from jax import lax
from jax.experimental import pallas as pl
from jax.experimental.pallas import tpu as pltpu
from jax.sharding import PartitionSpec as P

STEEPNESS = 4.0
THRESHOLD = 1.0
SHARPNESS = 12.0

BF = jnp.bfloat16
F32 = jnp.float32

W = 1024
NF = 192
LANES = 256
TAPS = 25
RIM = TAPS // 2
ROWS = 128
NK = 12
NFOC = 4
NDOSE = 4
TAP_ROWS = 112
GRID = 384
EDGE = 32
TEDGE = 16
GRAD_ROWS = 48
BAND_ROWS = 32


class Plan:
    def __init__(self, share, rows, order, turn):
        self.share = share
        self.rows = rows
        self.order = order
        self.turn = turn


OUTER = Plan(14, 16, 40, 1.91284375)
INNER = Plan(24, 24, 48, 1.62425)
PLANS = (OUTER, OUTER, INNER, INNER, INNER, INNER, OUTER, OUTER)
STARTS = tuple(sum(plan.share for plan in PLANS[:n]) - RIM for n in range(len(PLANS)))
WINDOW = (0, 1, 7, 2, 6, 3, 4, 5)


def low(table):
    return jnp.asarray(np.asarray(table, np.float32)).astype(BF)


def forward_table():
    phase = np.outer(np.arange(NF) - NF // 2, np.arange(W)) % W
    angle = 2.0 * math.pi * phase / W
    scale = 1.0 / math.sqrt(W)
    table = np.zeros((W, 2 * LANES))
    table[:, :NF] = scale * np.cos(angle).T
    table[:, LANES : LANES + NF] = -scale * np.sin(angle).T
    return table


def inverse_table():
    phase = np.outer(np.arange(NF) - NF // 2, np.arange(GRID)) % GRID
    angle = 2.0 * math.pi * phase / GRID
    scale = 1.0 / math.sqrt(W)
    table = np.zeros((2 * LANES, 2 * GRID))
    table[:NF, :GRID] = scale * np.cos(angle)
    table[:NF, GRID:] = scale * np.sin(angle)
    table[LANES : LANES + NF, :GRID] = -scale * np.sin(angle)
    table[LANES : LANES + NF, GRID:] = scale * np.cos(angle)
    return table


def interpolation_table():
    where = np.arange(W)[None, :] / W - np.arange(GRID)[:, None] / GRID
    orders = np.arange(1, NF)
    table = np.ones((GRID, W))
    for order in orders:
        table += 2.0 * np.cos(2.0 * math.pi * order * where)
    return table / GRID


def row_angles(order, left, right):
    return 2.0 * math.pi * (np.outer(np.arange(left), np.arange(right)) % order) / order


def complex_table(plan, angle):
    return plan.turn * np.block([[np.cos(angle), -np.sin(angle)], [np.sin(angle), np.cos(angle)]])


def tap_table(plan):
    u = plan.order
    table = complex_table(plan, row_angles(u, u, TAPS)).reshape(2, u, 2, TAPS)
    full = np.zeros((NFOC, 2, u, 2, TAP_ROWS))
    for focus in range(NFOC):
        full[focus, :, :, :, focus : TAPS * NFOC : NFOC] = table
    return full.reshape(NFOC * 2 * u, 2 * TAP_ROWS)


def window_table(plan):
    return complex_table(plan, -row_angles(plan.order, plan.order, plan.order))


def back_table(plan):
    angle = row_angles(plan.order, plan.order, plan.order)
    return plan.turn * np.concatenate([np.cos(angle), np.sin(angle)], axis=1)


def mix_table(plan, count=2):
    u, rows = plan.order, plan.rows
    table = complex_table(plan, row_angles(u, rows, u)).reshape(2, rows, 2, u)
    full = np.zeros((2, count, rows, count, 2, u))
    for q in range(count):
        full[:, q, :, q] = table
    return full.reshape(2 * count * rows, count * 2 * u)


def unmix_table(plan, count=4):
    u, rows = plan.order, plan.rows
    table = complex_table(plan, -row_angles(u, u, rows)).reshape(2, u, 2, rows)
    full = np.zeros((count, 2, u, 2, count, rows))
    for q in range(count):
        full[q, :, :, :, q] = table
    return full.reshape(count * 2 * u, 2 * count * rows)


def entry_table():
    parts = [forward_table()]
    places = {}
    first = W
    for plan in (INNER, OUTER):
        taps = tap_table(plan)
        half, width = taps.shape[0] // 2, taps.shape[1]
        part = np.zeros((half, 2 * LANES))
        part[:, :width] = taps[:half]
        part[:, LANES : LANES + width] = taps[half:]
        parts.append(part)
        places[plan] = slice(first, first + half)
        first += half
    return np.concatenate(parts), places


def row_tables():
    places = {}
    parts = []
    first = 0
    for plan in (INNER, OUTER):
        places[plan] = []
        for table in (window_table(plan), mix_table(plan), unmix_table(plan), back_table(plan)):
            rows, width = table.shape
            places[plan].append((slice(first, first + rows), slice(0, width)))
            part = np.zeros((-(-rows // 16) * 16, LANES))
            part[:rows, :width] = table
            parts.append(part)
            first += part.shape[0]
    return np.concatenate(parts), places


def placing_tables(count):
    grad = np.zeros((ROWS, count, GRAD_ROWS))
    band = np.zeros((ROWS, count, BAND_ROWS))
    for source in range(count):
        share, start = PLANS[WINDOW[source]].share, STARTS[WINDOW[source]]
        for row in range(share + 2 * RIM):
            if 0 <= start - RIM + row < ROWS:
                grad[start - RIM + row, source, row] = 1.0
        for row in range(share):
            if 0 <= start + row < ROWS:
                band[start + row, source, row] = 1.0
    return grad.reshape(ROWS, -1), band.reshape(ROWS, -1)


def dot(left, right):
    return jnp.dot(left, right, preferred_element_type=F32)


def here(values):
    corner = lax.axis_index("corner")
    value = jnp.int32(values[WINDOW[0]])
    for n in range(1, len(WINDOW)):
        value = jnp.where(corner == n, values[WINDOW[n]], value)
    return value


def by_plan(work):
    outer = here([int(plan is OUTER) for plan in PLANS]) == 1
    pl.when(outer)(lambda: work(OUTER))
    pl.when(jnp.logical_not(outer))(lambda: work(INNER))


def stacked(value):
    return jnp.concatenate([value[:, :LANES], value[:, LANES:]], axis=0).astype(BF)


def picked(count, length, first):
    row = lax.broadcasted_iota(jnp.int32, (count, length), 0) + first
    row = jnp.where(row >= length, row - length, row)
    column = lax.broadcasted_iota(jnp.int32, (count, length), 1)
    return jnp.where(row == column, 1.0, 0.0).astype(BF)


def edge_kernel(mask_ref, target_ref, dose_ref, out_ref, dose_rows_ref, mask_rows, target_rows, doses, sems):
    down = here(range(len(WINDOW))) < len(WINDOW) // 2
    mask_from = pl.multiple_of(jnp.where(down, ROWS - EDGE, 0), EDGE)
    target_from = pl.multiple_of(jnp.where(down, ROWS - TEDGE, 0), TEDGE)
    copies = [
        pltpu.make_async_copy(mask_ref.at[pl.ds(mask_from, EDGE)], mask_rows, sems.at[0]),
        pltpu.make_async_copy(target_ref.at[pl.ds(target_from, TEDGE)], target_rows, sems.at[1]),
        pltpu.make_async_copy(dose_ref, doses, sems.at[2]),
    ]
    for copy in copies:
        copy.start()
    for copy in copies:
        copy.wait()
    out_ref[:EDGE] = jnp.tanh(mask_rows[...]).astype(BF)
    out_ref[EDGE:] = target_rows[...].astype(F32).astype(BF)
    for d in range(NDOSE):
        dose_rows_ref[d : d + 1] = jnp.full((1, ROWS), doses[d])


def prepare_kernel(kernels_ref, mask_ref, entry_ref, hat_ref, spectra_ref, slope_ref, taps_ref, share_ref, sem):
    column = pl.multiple_of(lax.axis_index("corner") * ROWS, ROWS)
    share = jnp.tanh(mask_ref[:, pl.ds(column, ROWS)])
    share_ref[...] = 1.0 - share * share
    copy = pltpu.make_async_copy(share_ref, slope_ref, sem)
    copy.start()
    taps_ref[:, :, NFOC * TAPS - 4 :] = jnp.zeros((2, 2, TAP_ROWS - NFOC * TAPS + 4, 2 * NF), F32)
    places = entry_table()[1]

    def transform(plan):
        u = plan.order
        lane = lax.broadcasted_iota(jnp.int32, (TAP_ROWS, LANES), 1)
        table = jnp.concatenate(
            [
                entry_ref[places[plan], : 2 * TAP_ROWS],
                entry_ref[places[plan], LANES : LANES + 2 * TAP_ROWS],
            ],
            axis=0,
        )
        for kernel in range(0, NK, 2):
            slot = kernel // 2 % 2
            parts = []
            for q in range(2):
                for tap in range(TAPS):
                    taps_ref[slot, q, tap * NFOC : (tap + 1) * NFOC] = kernels_ref[kernel + q, tap]
                taps = taps_ref[slot, q]
                re = jnp.where(lane < NF, taps[:, :LANES], 0.0)
                im = jnp.where(lane < NF, pltpu.roll(taps, NF, 1)[:, :LANES], 0.0)
                parts.append(jnp.concatenate([re, im], axis=0).astype(BF))
            hats = dot(table, jnp.concatenate(parts, axis=1))
            for q in range(2):
                hat = hats[:, q * LANES : (q + 1) * LANES].reshape(NFOC, 2 * u, LANES)
                hat_ref[(kernel + q) * NFOC : (kernel + q + 1) * NFOC, : 2 * u] = hat

    by_plan(transform)
    field = jnp.tanh(mask_ref[...])
    spectra_ref[...] = dot(field.astype(BF), entry_ref[:W]).astype(BF)
    copy.wait()


def image_kernel(
    dose_ref,
    edge_ref,
    spectra_ref,
    target_ref,
    hat_ref,
    entry_ref,
    inverse_ref,
    interp_ref,
    forward_t_ref,
    inverse_t_ref,
    interp_t_ref,
    rows_ref,
    out_ref,
    mixed_ref,
    field_ref,
    aerial_ref,
    grad_ref,
    band_ref,
):
    places = row_tables()[1]

    def work(plan):
        u, count = plan.order, plan.rows
        scale = 1.0 / (plan.turn * plan.turn * plan.turn * u)
        window_rows, mix_rows, unmix_rows, back_rows = places[plan]
        start = here(STARTS)
        rows = spectra_ref[...]
        wanted = target_ref[...].astype(F32).astype(BF)
        first, first_wanted = start - RIM, start
        if plan is OUTER:
            rows = jnp.concatenate([dot(edge_ref[:EDGE], entry_ref[:W]).astype(BF), rows], axis=0)
            wanted = jnp.concatenate([edge_ref[EDGE:], wanted], axis=0)
            first, first_wanted = first + EDGE, first_wanted + TEDGE
        pick = picked(u, rows.shape[0], first)
        mask_hat = dot(rows_ref[window_rows], stacked(dot(pick, rows))) * scale
        mask_re = mask_hat[:u]
        mask_im = mask_hat[u:]
        band_ref[:count] = dot(picked(count, wanted.shape[0], first_wanted), wanted)
        for group in range(NFOC * NK // 4):
            stacks = []
            for pair in range(2):
                stack = []
                for q in range(2):
                    kernel = group * 4 + pair * 2 + q
                    hat = hat_ref[(kernel % NK) * NFOC + kernel // NK, : 2 * u]
                    stack.append(mask_re * hat[:u] - mask_im * hat[u:])
                    stack.append(mask_re * hat[u:] + mask_im * hat[:u])
                stacks.append(jnp.concatenate(stack, axis=0).astype(BF))
            mixed = dot(rows_ref[mix_rows], jnp.concatenate(stacks, axis=1))
            parts = []
            for pair in range(2):
                lanes = slice(pair * LANES, (pair + 1) * LANES)
                parts.append(jnp.concatenate([mixed[: 2 * count, lanes], mixed[2 * count :, lanes]], axis=1))
            mixed_ref[group * 4 * count : (group + 1) * 4 * count] = jnp.concatenate(parts, axis=0).astype(BF)
        per_focus = NK * count
        coarse = []
        for focus in range(NFOC):
            fields = dot(mixed_ref[focus * per_focus : (focus + 1) * per_focus], inverse_ref[...])
            field_ref[focus * per_focus : (focus + 1) * per_focus] = fields
            power = fields[:, :GRID] * fields[:, :GRID] + fields[:, GRID:] * fields[:, GRID:]
            summed = power[:count]
            for kernel in range(1, NK):
                summed = summed + power[kernel * count : (kernel + 1) * count]
            coarse.append(summed)
        coarse = jnp.concatenate(coarse, axis=0)
        coarse_high = coarse.astype(BF)
        coarse_low = (coarse - coarse_high.astype(F32)).astype(BF)
        both = dot(jnp.concatenate([coarse_high, coarse_low], axis=0), interp_ref[...])
        aerial_ref[: NFOC * count] = both[: NFOC * count] + both[NFOC * count :]
        local = lax.broadcasted_iota(jnp.int32, (count, ROWS), 0)
        pixel = lax.axis_index("tile") * ROWS + start + local
        valid = (local < plan.share) & (pixel >= 0) & (pixel < ROWS * lax.axis_size("tile"))
        valid = jnp.where(valid, 1.0, 0.0)
        doses = [dose_ref[d : d + 1] for d in range(NDOSE)]
        for chunk in range(W // ROWS):
            cols = slice(chunk * ROWS, (chunk + 1) * ROWS)
            high = None
            low_sum = None
            kept = []
            for focus in range(NFOC):
                aerial = aerial_ref[focus * count : (focus + 1) * count, cols]
                for d in range(NDOSE):
                    swing = jnp.tanh((0.5 * STEEPNESS * doses[d]) * aerial - 0.5 * STEEPNESS * THRESHOLD)
                    power = (0.5 * SHARPNESS / math.log(2.0)) * swing + 0.5 * SHARPNESS / math.log(2.0)
                    up = jnp.exp2(power)
                    down = jnp.exp2(-power)
                    high = up if high is None else high + up
                    low_sum = down if low_sum is None else low_sum + down
                    kept.append((swing, up, down))
            pixels = band_ref[:count, cols]
            top = jnp.log(high) / SHARPNESS
            bottom = -jnp.log(low_sum) / SHARPNESS
            band_ref[:count, cols] = top - bottom
            high_weight = valid * (top - pixels) / high
            low_weight = valid * (bottom - pixels) / low_sum
            for focus in range(NFOC):
                total = None
                for d in range(NDOSE):
                    swing, up, down = kept[focus * NDOSE + d]
                    term = (high_weight * up + low_weight * down) * (1.0 - swing * swing)
                    term = term * (0.5 * STEEPNESS * doses[d])
                    total = term if total is None else total + term
                grad_ref[focus * count : (focus + 1) * count, cols] = total
        coarse_grad = dot(grad_ref[: NFOC * count].astype(BF), interp_t_ref[...])
        acc_re = jnp.zeros((u, LANES), F32)
        acc_im = jnp.zeros((u, LANES), F32)
        for focus in range(NFOC):
            part = coarse_grad[focus * count : (focus + 1) * count]
            part = jnp.concatenate([part, part], axis=1)
            base = focus * per_focus
            field_grad = [
                part * field_ref[base + kernel * count : base + (kernel + 1) * count] for kernel in range(NK)
            ]
            mixed_grad = dot(jnp.concatenate(field_grad, axis=0).astype(BF), inverse_t_ref[...])
            grads = [
                stacked(mixed_grad[group * 4 * count : (group + 1) * 4 * count]) for group in range(NK // 4)
            ]
            grads = dot(rows_ref[unmix_rows], jnp.concatenate(grads, axis=1))
            for group in range(NK // 4):
                lanes = slice(group * LANES, (group + 1) * LANES)
                for q in range(4):
                    grad_re = grads[2 * q * u : (2 * q + 1) * u, lanes]
                    grad_im = grads[(2 * q + 1) * u : (2 * q + 2) * u, lanes]
                    hat = hat_ref[(group * 4 + q) * NFOC + focus, : 2 * u]
                    acc_re = acc_re + (grad_re * hat[:u] + grad_im * hat[u:])
                    acc_im = acc_im + (grad_im * hat[:u] - grad_re * hat[u:])
        acc_re = acc_re * scale
        acc_im = acc_im * scale
        acc = jnp.concatenate(
            [jnp.concatenate([acc_re, acc_im], axis=1), jnp.concatenate([-acc_im, acc_re], axis=1)], axis=0
        )
        spectra_grad = dot(rows_ref[back_rows], acc.astype(BF))
        if u < GRAD_ROWS:
            spectra_grad = jnp.concatenate([spectra_grad, jnp.zeros((GRAD_ROWS - u, 2 * LANES), F32)], axis=0)
        mask_grad = dot(spectra_grad.astype(BF), forward_t_ref[...]).astype(BF)
        empty = jnp.zeros((BAND_ROWS - count, ROWS), F32)
        for block in range(W // ROWS):
            cols = slice(block * ROWS, (block + 1) * ROWS)
            out_ref[block, :GRAD_ROWS] = mask_grad[:, cols]
            out_ref[block, GRAD_ROWS:] = jnp.concatenate([band_ref[:count, cols], empty], axis=0).astype(BF)

    by_plan(work)


def finish_kernel(blocks_ref, slope_ref, place_grad_ref, place_band_ref, band_ref, grad_ref):
    count = blocks_ref.shape[0]
    grads = blocks_ref[:, :GRAD_ROWS].reshape(count * GRAD_ROWS, ROWS)
    grad_ref[...] = dot(place_grad_ref[...], grads) * slope_ref[...]
    bands = blocks_ref[:, GRAD_ROWS:].reshape(count * BAND_ROWS, ROWS)
    band_ref[...] = dot(place_band_ref[...], bands)


def params(mib):
    return pltpu.CompilerParams(vmem_limit_bytes=mib << 20)


def whole(count):
    return [pl.BlockSpec(memory_space=pltpu.VMEM)] * count


def per_device(mask_logits, target, kernels, dose_levels):
    tiles = lax.axis_size("tile")
    corners = lax.axis_size("corner")
    edge, dose_rows = pl.pallas_call(
        edge_kernel,
        name="edge",
        out_shape=(
            jax.ShapeDtypeStruct((EDGE + TEDGE, W), BF),
            jax.ShapeDtypeStruct((NDOSE, ROWS), F32),
        ),
        in_specs=[pl.BlockSpec(memory_space=pl.ANY)] * 3,
        out_specs=tuple(whole(2)),
        scratch_shapes=[
            pltpu.VMEM((EDGE, W), F32),
            pltpu.VMEM((TEDGE, W), jnp.int32),
            pltpu.SMEM((NDOSE,), F32),
            pltpu.SemaphoreType.DMA((3,)),
        ],
        compiler_params=params(2),
        cost_estimate=pl.CostEstimate(flops=2_000_000_000, bytes_accessed=0, transcendentals=0),
    )(*[pltpu.with_memory_space_constraint(x, pltpu.HBM) for x in (mask_logits, target, dose_levels)])
    pairs = []
    for i in range(tiles - 1):
        for c in range(corners):
            begin = STARTS[WINDOW[c]] - RIM
            if begin < 0:
                pairs.append((i * corners + c, (i + 1) * corners + c))
            elif begin + PLANS[WINDOW[c]].share + 2 * RIM > ROWS:
                pairs.append(((i + 1) * corners + c, i * corners + c))
    edge = lax.ppermute(edge, ("tile", "corner"), pairs)
    entry = low(entry_table()[0])
    inverse = low(inverse_table())
    interp = low(interpolation_table())
    count = NFOC * NK
    hats, spectra, slope = pl.pallas_call(
        prepare_kernel,
        name="prepare",
        out_shape=(
            jax.ShapeDtypeStruct((count, 2 * INNER.order, LANES), F32),
            jax.ShapeDtypeStruct((ROWS, 2 * LANES), BF),
            jax.ShapeDtypeStruct((ROWS, ROWS), F32),
        ),
        in_specs=whole(3),
        out_specs=tuple(whole(2)) + (pl.BlockSpec(memory_space=pltpu.HBM),),
        scratch_shapes=[
            pltpu.VMEM((2, 2, TAP_ROWS, 2 * NF), F32),
            pltpu.VMEM((ROWS, ROWS), F32),
            pltpu.SemaphoreType.DMA,
        ],
        compiler_params=params(6),
        cost_estimate=pl.CostEstimate(flops=1_200_000_000, bytes_accessed=0, transcendentals=0),
    )(kernels.transpose(1, 2, 0, 3), mask_logits, entry)
    blocks = pl.pallas_call(
        image_kernel,
        name="image",
        out_shape=jax.ShapeDtypeStruct((W // ROWS, GRAD_ROWS + BAND_ROWS, ROWS), BF),
        in_specs=whole(12),
        out_specs=pl.BlockSpec(memory_space=pltpu.VMEM),
        scratch_shapes=[
            pltpu.VMEM((count * INNER.rows, 2 * LANES), BF),
            pltpu.VMEM((count * INNER.rows, 2 * GRID), F32),
            pltpu.VMEM((NFOC * INNER.rows, W), F32),
            pltpu.VMEM((NFOC * INNER.rows, W), F32),
            pltpu.VMEM((INNER.rows, W), F32),
        ],
        compiler_params=params(14),
        cost_estimate=pl.CostEstimate(flops=4_000_000_000, bytes_accessed=8_000_000, transcendentals=0),
    )(
        dose_rows,
        edge,
        spectra,
        target,
        hats,
        entry,
        inverse,
        interp,
        low(forward_table().T),
        low(inverse_table().T),
        low(interpolation_table().T),
        low(row_tables()[0]),
    )
    place_grad, place_band = placing_tables(corners)
    blocks = lax.all_to_all(blocks, "corner", 0, 0, tiled=True)
    return pl.pallas_call(
        finish_kernel,
        name="finish",
        out_shape=(
            jax.ShapeDtypeStruct((ROWS, ROWS), F32),
            jax.ShapeDtypeStruct((ROWS, ROWS), F32),
        ),
        in_specs=whole(4),
        out_specs=tuple(whole(2)),
        compiler_params=params(4),
    )(blocks, slope, low(place_grad), low(place_band))


def solution(mesh):
    return jax.shard_map(
        per_device,
        mesh=mesh,
        in_specs=(P("tile", None), P("tile", None), P(), P()),
        out_specs=(P("tile", "corner"), P("tile", "corner")),
        check_vma=False,
    )
```

time: 31.8 us -> 30.6 us (0.962)
  Pallas kernels: 10.1 us -> 8.99 us
    pallas_call x1, Pallas kernels: 6.8 us -> 5.62 us  [per_device(): pl.pallas_call(image_kernel, name='image', out_shape=jax.ShapeDtypeStruct...]
  transfers between devices with their start and end apart: 1 -> 1, of which waited for: 1 -> 1; matrix products, arithmetic and copies ran while one was open for 0% -> 0% of each run, Pallas kernels for 4% -> 5%
where the time goes in v4:
time: 30.6 us; the launch traced here: 30.5 us
  blocking collectives  12.5 us (41%)
  Pallas kernels  8.99 us (29%)
  waiting for transfers between devices  6.04 us (20%)
  starting transfers between devices  2.05 us (7%)
  between operations  0.82 us (3%)
    all_to_all x1, blocking collectives, per_device(): blocks = lax.all_to_all(blocks, 'corner', 0, 0, tiled=True)  12.5 us
    ppermute x1, waiting for transfers between devices, per_device(): edge = lax.ppermute(edge, ('tile', 'corner'), pairs)  6.04 us
    pallas_call x1, Pallas kernels, per_device(): pl.pallas_call(image_kernel, name='image', out_shape=jax.ShapeDtypeStruct...  5.62 us
    ppermute x1, starting transfers between devices, per_device(): edge = lax.ppermute(edge, ('tile', 'corner'), pairs)  2.05 us
    pallas_call x1, Pallas kernels, per_device(): pl.pallas_call(prepare_kernel, name='prepare', out_shape=(jax.ShapeDtypeS...  1.4 us
    pallas_call x1, Pallas kernels, per_device(): pl.pallas_call(edge_kernel, name='edge', out_shape=(jax.ShapeDtypeStruct(...  1.13 us
    pallas_call x1, Pallas kernels, per_device(): pl.pallas_call(finish_kernel, name='finish', out_shape=(jax.ShapeDtypeStr...  0.84 us
  transfers between devices with their start and end apart: 1, of which 1 were waited for; matrix products, arithmetic and copies ran while one was open for 0% of the time, Pallas kernels for 5%

profile of v4, /device:TPU:2, one launch (start us, length us, event | category | flops | bytes accessed | tf_op | source)
XLA Modules:
  0.0 30.5 jit_solution(4226412810912214859)
XLA Ops:
  0.6 0.0 copy-start.5
  0.6 0.0 copy-start.3
  0.7 0.0 copy-start.2
  0.7 0.0 copy-start.10
  0.7 0.0 copy-start.11
  0.7 1.1 %edge.1 = (bf16[48,1024]{1,0:T(8,128)(2,1)S(1)}, f32[4,128]{1,0:T(4,128)S(1)}) custom-call(f32[128,1024]{1,0:T(8,128)} %mask_ref.3, s32[128,1024]{1,0:T(8,128)} %target_ref.3, f32[4]{0:T(128)} %dose_ref.1), custom_call_target="tpu_custom_call" | custom-call | flops 2000000000 | tf_op jit(solution)/shard_map/edge/pallas_call | solution.py:427
  1.8 2.1 %collective-permute-start = (bf16[48,1024]{1,0:T(8,128)(2,1)S(1)}, bf16[48,1024]{1,0:T(8,128)(2,1)S(1)}, u32[]{:S(2)}, u32[]{:S(2)}) collective-permute-start(bf16[48,1024]{1,0:T(8,128)(2,1)S(1)} %get-tuple-element.8), channel_id=1, source_target_pairs={{0,8},{1,9},{10,2},{12,4},{8,16},{9,17},{18,10},{20,12},{16,24},{1... | collective-permute-start | bytes 294920 | tf_op jit(solution)/shard_map/ppermute | solution.py:453
  3.9 0.0 copy-done.5
  3.9 0.0 copy-done.3
  3.9 0.0 copy-done.2
  3.9 0.0 copy-start.4
  3.9 0.0 copy-start.6
  3.9 0.0 copy-start.7
  4.0 0.0 copy-start.8
  4.0 0.0 copy-start.9
  4.0 1.4 %prepare.1 = (f32[48,96,256]{2,1,0:T(8,128)S(1)}, bf16[128,512]{1,0:T(8,128)(2,1)S(1)}, f32[128,128]{1,0:T(8,128)S(1)}) custom-call(f32[12,25,4,384]{3,2,1,0:T(4,128)S(1)} %bitcast.1, f32[128,1024]{1,0:T(8,128)S(1)} %copy-done.3, bf16[1376,512]{1,0:T(8,128)(2,1)S(1)} %copy-done.5), custom_call_target="tpu_custom_call" | custom-call | flops 1200000000 | tf_op jit(solution)/shard_map/prepare/pallas_call | solution.py:458
  5.4 6.0 %collective-permute-done.edge_ref = bf16[48,1024]{1,0:T(8,128)(2,1)S(1)} collective-permute-done((bf16[48,1024]{1,0:T(8,128)(2,1)S(1)}, bf16[48,1024]{1,0:T(8,128)(2,1)S(1)}, u32[]{:S(2)}, u32[]{:S(2)}) %collective-permute-start) | collective-permute-done | bytes 98336 | tf_op jit(solution)/shard_map/ppermute | solution.py:453
  11.4 0.0 copy-done.10
  11.4 0.0 copy-done.11
  11.4 0.0 copy-done.4
  11.4 0.0 copy-done.6
  11.4 0.0 copy-done.7
  11.5 0.0 copy-done.8
  11.5 0.0 copy-done.9
  11.5 0.0 copy-start
  11.5 0.0 copy-start.1
  11.5 5.6 %image.1 = bf16[8,80,128]{2,1,0:T(8,128)(2,1)S(1)} custom-call(f32[4,128]{1,0:T(4,128)S(1)} %get-tuple-element.7.dose_ref, bf16[48,1024]{1,0:T(8,128)(2,1)S(1)} %collective-permute-done.edge_ref, bf16[128,512]{1,0:T(8,128)(2,1)S(1)} %get-tuple-element.9.spectra_ref, s32[128,1024]{1,0:T(8,128)S(1)} %copy-done.4, ...), custom_call_target="tpu_custom_call" | custom-call | flops 4000000000 | bytes 8000000 | tf_op jit(solution)/shard_map/image/pallas_call | solution.py:476
  17.1 12.5 %all_to_all.5.blocks_ref = bf16[8,80,128]{2,1,0:T(8,128)(2,1)S(1)} all-to-all(bf16[8,80,128]{2,1,0:T(8,128)(2,1)S(1)} %image.1), channel_id=1, replica_groups=mesh['tile'=32,'corner'=8] {'corner'}, dimensions={0} | all-to-all | bytes 327680 | tf_op jit(solution)/shard_map/all_to_all | solution.py:506
  29.6 0.0 copy-done
  29.6 0.0 copy-done.1
  29.6 0.8 %finish.1 = (f32[128,128]{1,0:T(8,128)}, f32[128,128]{1,0:T(8,128)}) custom-call(bf16[8,80,128]{2,1,0:T(8,128)(2,1)S(1)} %all_to_all.5.blocks_ref, f32[128,128]{1,0:T(8,128)S(1)} %get-tuple-element.11.slope_ref, bf16[128,384]{1,0:T(8,128)(2,1)S(1)} %copy-done, bf16[128,256]{1,0:T(8,128)(2,1)S(1)} %copy-done.1), custom_call_target="tpu_custom_call" | custom-call | tf_op jit(solution)/shard_map/finish/pallas_call | solution.py:507
Async XLA Ops:
  0.6 3.3 %copy-start.5 = (bf16[1376,512]{1,0:T(8,128)(2,1)S(1)}, bf16[1376,512]{1,0:T(8,128)(2,1)}, u32[]{:S(2)}) copy-start(bf16[1376,512]{1,0:T(8,128)(2,1)} %constant.27.entry_ref) | copy-start | bytes 4227076
  0.6 3.3 %copy-start.3 = (f32[128,1024]{1,0:T(8,128)S(1)}, f32[128,1024]{1,0:T(8,128)}, u32[]{:S(2)}) copy-start(f32[128,1024]{1,0:T(8,128)} %mask_ref.3) | copy-start | bytes 1572868
  0.7 3.3 %copy-start.2 = (f32[4,12,25,384]{3,0,2,1:T(4,128)S(1)}, f32[4,12,25,384]{3,0,2,1:T(4,128)}, u32[]{:S(2)}) copy-start(f32[4,12,25,384]{3,0,2,1:T(4,128)} %param.15) | copy-start | bytes 5529604
  0.7 10.8 %copy-start.10 = (bf16[512,768]{1,0:T(8,128)(2,1)S(1)}, bf16[512,768]{1,0:T(8,128)(2,1)}, u32[]{:S(2)}) copy-start(bf16[512,768]{1,0:T(8,128)(2,1)} %constant.28.inverse_ref) | copy-start | bytes 2359300
  0.7 10.8 %copy-start.11 = (bf16[1136,256]{1,0:T(8,128)(2,1)S(1)}, bf16[1136,256]{1,0:T(8,128)(2,1)}, u32[]{:S(2)}) copy-start(bf16[1136,256]{1,0:T(8,128)(2,1)} %constant.33.rows_ref) | copy-start | bytes 1744900
  1.8 9.6 %collective-permute-start = (bf16[48,1024]{1,0:T(8,128)(2,1)S(1)}, bf16[48,1024]{1,0:T(8,128)(2,1)S(1)}, u32[]{:S(2)}, u32[]{:S(2)}) collective-permute-start(bf16[48,1024]{1,0:T(8,128)(2,1)S(1)} %get-tuple-element.8), channel_id=1, source_target_pairs={{0,8},{1,9},{10,2},{12,4},{8,16},{9,17},{18,10},{20,12},{16,24},{1... | collective-permute-start | bytes 294920 | tf_op jit(solution)/shard_map/ppermute | solution.py:453
  3.9 7.5 %copy-start.4 = (s32[128,1024]{1,0:T(8,128)S(1)}, s32[128,1024]{1,0:T(8,128)}, u32[]{:S(2)}) copy-start(s32[128,1024]{1,0:T(8,128)} %target_ref.3) | copy-start | bytes 1572868
  3.9 7.5 %copy-start.6 = (bf16[512,1024]{1,0:T(8,128)(2,1)S(1)}, bf16[512,1024]{1,0:T(8,128)(2,1)}, u32[]{:S(2)}) copy-start(bf16[512,1024]{1,0:T(8,128)(2,1)} %constant.30.forward_t_ref) | copy-start | bytes 3145732
  3.9 7.5 %copy-start.7 = (bf16[1024,384]{1,0:T(8,128)(2,1)S(1)}, bf16[1024,384]{1,0:T(8,128)(2,1)}, u32[]{:S(2)}) copy-start(bf16[1024,384]{1,0:T(8,128)(2,1)} %constant.32.interp_t_ref) | copy-start | bytes 2359300
  4.0 7.5 %copy-start.8 = (bf16[768,512]{1,0:T(8,128)(2,1)S(1)}, bf16[768,512]{1,0:T(8,128)(2,1)}, u32[]{:S(2)}) copy-start(bf16[768,512]{1,0:T(8,128)(2,1)} %constant.31.inverse_t_ref) | copy-start | bytes 2359300
  4.0 7.5 %copy-start.9 = (bf16[384,1024]{1,0:T(8,128)(2,1)S(1)}, bf16[384,1024]{1,0:T(8,128)(2,1)}, u32[]{:S(2)}) copy-start(bf16[384,1024]{1,0:T(8,128)(2,1)} %constant.29.interp_ref) | copy-start | bytes 2359300
  11.5 18.2 %copy-start = (bf16[128,384]{1,0:T(8,128)(2,1)S(1)}, bf16[128,384]{1,0:T(8,128)(2,1)}, u32[]{:S(2)}) copy-start(bf16[128,384]{1,0:T(8,128)(2,1)} %constant.34.place_grad_ref) | copy-start | bytes 294916
  11.5 18.2 %copy-start.1 = (bf16[128,256]{1,0:T(8,128)(2,1)S(1)}, bf16[128,256]{1,0:T(8,128)(2,1)}, u32[]{:S(2)}) copy-start(bf16[128,256]{1,0:T(8,128)(2,1)} %constant.35.place_band_ref) | copy-start | bytes 196612

commit v5 on v4

--- a/solution.py
+++ b/solution.py
@@ -61,25 +61,28 @@
     return table
 
 
+def half_grid():
+    return (np.arange(GRID // 2) + 0.5) / GRID
+
+
 def inverse_table():
-    phase = np.outer(np.arange(NF) - NF // 2, np.arange(GRID)) % GRID
-    angle = 2.0 * math.pi * phase / GRID
+    angle = 2.0 * math.pi * np.outer(np.arange(NF) - NF // 2, half_grid())
     scale = 1.0 / math.sqrt(W)
-    table = np.zeros((2 * LANES, 2 * GRID))
-    table[:NF, :GRID] = scale * np.cos(angle)
-    table[:NF, GRID:] = scale * np.sin(angle)
-    table[LANES : LANES + NF, :GRID] = -scale * np.sin(angle)
-    table[LANES : LANES + NF, GRID:] = scale * np.cos(angle)
+    table = np.zeros((LANES, 2 * LANES))
+    table[:NF, : GRID // 2] = scale * np.cos(angle)
+    table[:NF, LANES : LANES + GRID // 2] = scale * np.sin(angle)
     return table
 
 
 def interpolation_table():
-    where = np.arange(W)[None, :] / W - np.arange(GRID)[:, None] / GRID
-    orders = np.arange(1, NF)
-    table = np.ones((GRID, W))
-    for order in orders:
-        table += 2.0 * np.cos(2.0 * math.pi * order * where)
-    return table / GRID
+    table = np.zeros((2 * LANES, W))
+    for first, points in ((0, half_grid()), (LANES, -half_grid())):
+        where = np.arange(W)[None, :] / W - points[:, None]
+        part = np.ones(where.shape)
+        for order in range(1, NF):
+            part += 2.0 * np.cos(2.0 * math.pi * order * where)
+        table[first : first + GRID // 2] = part / GRID
+    return table
 
 
 def row_angles(order, left, right):
@@ -310,21 +313,29 @@
                     stack.append(mask_re * hat[u:] + mask_im * hat[:u])
                 stacks.append(jnp.concatenate(stack, axis=0).astype(BF))
             mixed = dot(rows_ref[mix_rows], jnp.concatenate(stacks, axis=1))
-            parts = []
-            for pair in range(2):
-                lanes = slice(pair * LANES, (pair + 1) * LANES)
-                parts.append(jnp.concatenate([mixed[: 2 * count, lanes], mixed[2 * count :, lanes]], axis=1))
-            mixed_ref[group * 4 * count : (group + 1) * 4 * count] = jnp.concatenate(parts, axis=0).astype(BF)
-        per_focus = NK * count
+            half = 2 * count
+            parts = [mixed[:half, :LANES], mixed[:half, LANES:], mixed[half:, :LANES], mixed[half:, LANES:]]
+            mixed_ref[group * 8 * count : (group + 1) * 8 * count] = jnp.concatenate(parts, axis=0).astype(BF)
+        per_focus = 2 * NK * count
+        slots = [
+            (group * 8 * count + q * count, group * 8 * count + (4 + q) * count)
+            for group in range(NK // 4)
+            for q in range(4)
+        ]
         coarse = []
         for focus in range(NFOC):
             fields = dot(mixed_ref[focus * per_focus : (focus + 1) * per_focus], inverse_ref[...])
             field_ref[focus * per_focus : (focus + 1) * per_focus] = fields
-            power = fields[:, :GRID] * fields[:, :GRID] + fields[:, GRID:] * fields[:, GRID:]
-            summed = power[:count]
-            for kernel in range(1, NK):
-                summed = summed + power[kernel * count : (kernel + 1) * count]
-            coarse.append(summed)
+            squares = jnp.zeros((count, 2 * LANES), F32)
+            cross = jnp.zeros((count, LANES), F32)
+            for at_re, at_im in slots:
+                re = fields[at_re : at_re + count]
+                im = fields[at_im : at_im + count]
+                squares = squares + (re * re + im * im)
+                cross = cross + (im[:, :LANES] * re[:, LANES:] - re[:, :LANES] * im[:, LANES:])
+            squares = squares[:, :LANES] + squares[:, LANES:]
+            cross = 2.0 * cross
+            coarse.append(jnp.concatenate([squares + cross, squares - cross], axis=1))
         coarse = jnp.concatenate(coarse, axis=0)
         coarse_high = coarse.astype(BF)
         coarse_low = (coarse - coarse_high.astype(F32)).astype(BF)
@@ -367,18 +378,28 @@
         coarse_grad = dot(grad_ref[: NFOC * count].astype(BF), interp_t_ref[...])
         acc_re = jnp.zeros((u, LANES), F32)
         acc_im = jnp.zeros((u, LANES), F32)
+        stacks = []
         for focus in range(NFOC):
             part = coarse_grad[focus * count : (focus + 1) * count]
-            part = jnp.concatenate([part, part], axis=1)
+            both = part[:, :LANES] + part[:, LANES:]
+            apart = part[:, :LANES] - part[:, LANES:]
+            both = jnp.concatenate([both, both], axis=1)
+            apart = jnp.concatenate([-apart, apart], axis=1)
             base = focus * per_focus
-            field_grad = [
-                part * field_ref[base + kernel * count : base + (kernel + 1) * count] for kernel in range(NK)
-            ]
-            mixed_grad = dot(jnp.concatenate(field_grad, axis=0).astype(BF), inverse_t_ref[...])
-            grads = [
-                stacked(mixed_grad[group * 4 * count : (group + 1) * 4 * count]) for group in range(NK // 4)
-            ]
-            grads = dot(rows_ref[unmix_rows], jnp.concatenate(grads, axis=1))
+            field_grad = {}
+            for at_re, at_im in slots:
+                re = field_ref[base + at_re : base + at_re + count]
+                im = field_ref[base + at_im : base + at_im + count]
+                re_turned = jnp.concatenate([re[:, LANES:], re[:, :LANES]], axis=1)
+                im_turned = jnp.concatenate([im[:, LANES:], im[:, :LANES]], axis=1)
+                field_grad[at_re] = both * re + apart * im_turned
+                field_grad[at_im] = both * im - apart * re_turned
+            field_grad = jnp.concatenate([field_grad[at] for at in sorted(field_grad)], axis=0)
+            mixed_grad = dot(field_grad.astype(BF), inverse_t_ref[...]).astype(BF)
+            grads = [mixed_grad[group * 8 * count : (group + 1) * 8 * count] for group in range(NK // 4)]
+            stacks.append(jnp.concatenate(grads, axis=1))
+        for focus in range(NFOC):
+            grads = dot(rows_ref[unmix_rows], stacks[focus])
             for group in range(NK // 4):
                 lanes = slice(group * LANES, (group + 1) * LANES)
                 for q in range(4):
@@ -480,8 +501,8 @@
         in_specs=whole(12),
         out_specs=pl.BlockSpec(memory_space=pltpu.VMEM),
         scratch_shapes=[
-            pltpu.VMEM((count * INNER.rows, 2 * LANES), BF),
-            pltpu.VMEM((count * INNER.rows, 2 * GRID), F32),
+            pltpu.VMEM((2 * count * INNER.rows, LANES), BF),
+            pltpu.VMEM((2 * count * INNER.rows, 2 * LANES), F32),
             pltpu.VMEM((NFOC * INNER.rows, W), F32),
             pltpu.VMEM((NFOC * INNER.rows, W), F32),
             pltpu.VMEM((INNER.rows, W), F32),

time: 30.6 us -> 29.8 us (0.974)
  Pallas kernels: 8.99 us -> 8.15 us
    pallas_call x1, Pallas kernels: 5.62 us -> 4.78 us  [per_device(): pl.pallas_call(image_kernel, name='image', out_shape=jax.ShapeDtypeStruct...]
where the time goes in v5:
time: 29.8 us; the launch traced here: 29.6 us
  blocking collectives  12.5 us (42%)
  Pallas kernels  8.15 us (27%)
  waiting for transfers between devices  6.04 us (20%)
  starting transfers between devices  2.05 us (7%)
  between operations  0.82 us (3%)
    all_to_all x1, blocking collectives, per_device(): blocks = lax.all_to_all(blocks, 'corner', 0, 0, tiled=True)  12.5 us
    ppermute x1, waiting for transfers between devices, per_device(): edge = lax.ppermute(edge, ('tile', 'corner'), pairs)  6.04 us
    pallas_call x1, Pallas kernels, per_device(): pl.pallas_call(image_kernel, name='image', out_shape=jax.ShapeDtypeStruct...  4.78 us
    ppermute x1, starting transfers between devices, per_device(): edge = lax.ppermute(edge, ('tile', 'corner'), pairs)  2.05 us
    pallas_call x1, Pallas kernels, per_device(): pl.pallas_call(prepare_kernel, name='prepare', out_shape=(jax.ShapeDtypeS...  1.4 us
    pallas_call x1, Pallas kernels, per_device(): pl.pallas_call(edge_kernel, name='edge', out_shape=(jax.ShapeDtypeStruct(...  1.13 us
    pallas_call x1, Pallas kernels, per_device(): pl.pallas_call(finish_kernel, name='finish', out_shape=(jax.ShapeDtypeStr...  0.84 us
  transfers between devices with their start and end apart: 1, of which 1 were waited for; matrix products, arithmetic and copies ran while one was open for 0% of the time, Pallas kernels for 5%

profile of v5, /device:TPU:2, one launch (start us, length us, event | category | flops | bytes accessed | tf_op | source)
XLA Modules:
  0.0 29.6 jit_solution(2746492276717913321)
XLA Ops:
  0.6 0.0 copy-start.5
  0.6 0.0 copy-start.3
  0.7 0.0 copy-start.2
  0.7 0.0 copy-start.10
  0.7 0.0 copy-start.11
  0.7 1.1 %edge.1 = (bf16[48,1024]{1,0:T(8,128)(2,1)S(1)}, f32[4,128]{1,0:T(4,128)S(1)}) custom-call(f32[128,1024]{1,0:T(8,128)} %mask_ref.3, s32[128,1024]{1,0:T(8,128)} %target_ref.3, f32[4]{0:T(128)} %dose_ref.1), custom_call_target="tpu_custom_call" | custom-call | flops 2000000000 | tf_op jit(solution)/shard_map/edge/pallas_call | solution.py:448
  1.8 2.1 %collective-permute-start = (bf16[48,1024]{1,0:T(8,128)(2,1)S(1)}, bf16[48,1024]{1,0:T(8,128)(2,1)S(1)}, u32[]{:S(2)}, u32[]{:S(2)}) collective-permute-start(bf16[48,1024]{1,0:T(8,128)(2,1)S(1)} %get-tuple-element.8), channel_id=1, source_target_pairs={{0,8},{1,9},{10,2},{12,4},{8,16},{9,17},{18,10},{20,12},{16,24},{1... | collective-permute-start | bytes 294920 | tf_op jit(solution)/shard_map/ppermute | solution.py:474
  3.9 0.0 copy-done.5
  3.9 0.0 copy-done.3
  3.9 0.0 copy-done.2
  3.9 0.0 copy-start.4
  3.9 0.0 copy-start.6
  3.9 0.0 copy-start.7
  4.0 0.0 copy-start.8
  4.0 0.0 copy-start.9
  4.0 1.4 %prepare.1 = (f32[48,96,256]{2,1,0:T(8,128)S(1)}, bf16[128,512]{1,0:T(8,128)(2,1)S(1)}, f32[128,128]{1,0:T(8,128)S(1)}) custom-call(f32[12,25,4,384]{3,2,1,0:T(4,128)S(1)} %bitcast.1, f32[128,1024]{1,0:T(8,128)S(1)} %copy-done.3, bf16[1376,512]{1,0:T(8,128)(2,1)S(1)} %copy-done.5), custom_call_target="tpu_custom_call" | custom-call | flops 1200000000 | tf_op jit(solution)/shard_map/prepare/pallas_call | solution.py:479
  5.4 6.0 %collective-permute-done.edge_ref = bf16[48,1024]{1,0:T(8,128)(2,1)S(1)} collective-permute-done((bf16[48,1024]{1,0:T(8,128)(2,1)S(1)}, bf16[48,1024]{1,0:T(8,128)(2,1)S(1)}, u32[]{:S(2)}, u32[]{:S(2)}) %collective-permute-start) | collective-permute-done | bytes 98336 | tf_op jit(solution)/shard_map/ppermute | solution.py:474
  11.4 0.0 copy-done.10
  11.4 0.0 copy-done.11
  11.4 0.0 copy-done.4
  11.4 0.0 copy-done.6
  11.4 0.0 copy-done.7
  11.5 0.0 copy-done.8
  11.5 0.0 copy-done.9
  11.5 0.0 copy-start
  11.5 0.0 copy-start.1
  11.5 4.8 %image.1 = bf16[8,80,128]{2,1,0:T(8,128)(2,1)S(1)} custom-call(f32[4,128]{1,0:T(4,128)S(1)} %get-tuple-element.7.dose_ref, bf16[48,1024]{1,0:T(8,128)(2,1)S(1)} %collective-permute-done.edge_ref, bf16[128,512]{1,0:T(8,128)(2,1)S(1)} %get-tuple-element.9.spectra_ref, s32[128,1024]{1,0:T(8,128)S(1)} %copy-done.4, ...), custom_call_target="tpu_custom_call" | custom-call | flops 4000000000 | bytes 8000000 | tf_op jit(solution)/shard_map/image/pallas_call | solution.py:497
  16.3 12.5 %all_to_all.5.blocks_ref = bf16[8,80,128]{2,1,0:T(8,128)(2,1)S(1)} all-to-all(bf16[8,80,128]{2,1,0:T(8,128)(2,1)S(1)} %image.1), channel_id=1, replica_groups=mesh['tile'=32,'corner'=8] {'corner'}, dimensions={0} | all-to-all | bytes 327680 | tf_op jit(solution)/shard_map/all_to_all | solution.py:527
  28.8 0.0 copy-done
  28.8 0.0 copy-done.1
  28.8 0.8 %finish.1 = (f32[128,128]{1,0:T(8,128)}, f32[128,128]{1,0:T(8,128)}) custom-call(bf16[8,80,128]{2,1,0:T(8,128)(2,1)S(1)} %all_to_all.5.blocks_ref, f32[128,128]{1,0:T(8,128)S(1)} %get-tuple-element.11.slope_ref, bf16[128,384]{1,0:T(8,128)(2,1)S(1)} %copy-done, bf16[128,256]{1,0:T(8,128)(2,1)S(1)} %copy-done.1), custom_call_target="tpu_custom_call" | custom-call | tf_op jit(solution)/shard_map/finish/pallas_call | solution.py:528
Async XLA Ops:
  0.6 3.3 %copy-start.5 = (bf16[1376,512]{1,0:T(8,128)(2,1)S(1)}, bf16[1376,512]{1,0:T(8,128)(2,1)}, u32[]{:S(2)}) copy-start(bf16[1376,512]{1,0:T(8,128)(2,1)} %constant.27.entry_ref) | copy-start | bytes 4227076
  0.6 3.3 %copy-start.3 = (f32[128,1024]{1,0:T(8,128)S(1)}, f32[128,1024]{1,0:T(8,128)}, u32[]{:S(2)}) copy-start(f32[128,1024]{1,0:T(8,128)} %mask_ref.3) | copy-start | bytes 1572868
  0.7 3.3 %copy-start.2 = (f32[4,12,25,384]{3,0,2,1:T(4,128)S(1)}, f32[4,12,25,384]{3,0,2,1:T(4,128)}, u32[]{:S(2)}) copy-start(f32[4,12,25,384]{3,0,2,1:T(4,128)} %param.15) | copy-start | bytes 5529604
  0.7 10.8 %copy-start.10 = (bf16[512,256]{1,0:T(8,128)(2,1)S(1)}, bf16[512,256]{1,0:T(8,128)(2,1)}, u32[]{:S(2)}) copy-start(bf16[512,256]{1,0:T(8,128)(2,1)} %constant.31.inverse_t_ref) | copy-start | bytes 786436
  0.7 10.8 %copy-start.11 = (bf16[256,512]{1,0:T(8,128)(2,1)S(1)}, bf16[256,512]{1,0:T(8,128)(2,1)}, u32[]{:S(2)}) copy-start(bf16[256,512]{1,0:T(8,128)(2,1)} %constant.28.inverse_ref) | copy-start | bytes 786436
  1.8 9.6 %collective-permute-start = (bf16[48,1024]{1,0:T(8,128)(2,1)S(1)}, bf16[48,1024]{1,0:T(8,128)(2,1)S(1)}, u32[]{:S(2)}, u32[]{:S(2)}) collective-permute-start(bf16[48,1024]{1,0:T(8,128)(2,1)S(1)} %get-tuple-element.8), channel_id=1, source_target_pairs={{0,8},{1,9},{10,2},{12,4},{8,16},{9,17},{18,10},{20,12},{16,24},{1... | collective-permute-start | bytes 294920 | tf_op jit(solution)/shard_map/ppermute | solution.py:474
  3.9 7.5 %copy-start.4 = (s32[128,1024]{1,0:T(8,128)S(1)}, s32[128,1024]{1,0:T(8,128)}, u32[]{:S(2)}) copy-start(s32[128,1024]{1,0:T(8,128)} %target_ref.3) | copy-start | bytes 1572868
  3.9 7.5 %copy-start.6 = (bf16[1024,512]{1,0:T(8,128)(2,1)S(1)}, bf16[1024,512]{1,0:T(8,128)(2,1)}, u32[]{:S(2)}) copy-start(bf16[1024,512]{1,0:T(8,128)(2,1)} %constant.32.interp_t_ref) | copy-start | bytes 3145732
  3.9 7.5 %copy-start.7 = (bf16[512,1024]{1,0:T(8,128)(2,1)S(1)}, bf16[512,1024]{1,0:T(8,128)(2,1)}, u32[]{:S(2)}) copy-start(bf16[512,1024]{1,0:T(8,128)(2,1)} %constant.30.forward_t_ref) | copy-start | bytes 3145732
  4.0 7.5 %copy-start.8 = (bf16[512,1024]{1,0:T(8,128)(2,1)S(1)}, bf16[512,1024]{1,0:T(8,128)(2,1)}, u32[]{:S(2)}) copy-start(bf16[512,1024]{1,0:T(8,128)(2,1)} %constant.29.interp_ref) | copy-start | bytes 3145732
  4.0 7.5 %copy-start.9 = (bf16[1136,256]{1,0:T(8,128)(2,1)S(1)}, bf16[1136,256]{1,0:T(8,128)(2,1)}, u32[]{:S(2)}) copy-start(bf16[1136,256]{1,0:T(8,128)(2,1)} %constant.33.rows_ref) | copy-start | bytes 1744900
  11.5 17.3 %copy-start = (bf16[128,384]{1,0:T(8,128)(2,1)S(1)}, bf16[128,384]{1,0:T(8,128)(2,1)}, u32[]{:S(2)}) copy-start(bf16[128,384]{1,0:T(8,128)(2,1)} %constant.34.place_grad_ref) | copy-start | bytes 294916
  11.5 17.3 %copy-start.1 = (bf16[128,256]{1,0:T(8,128)(2,1)S(1)}, bf16[128,256]{1,0:T(8,128)(2,1)}, u32[]{:S(2)}) copy-start(bf16[128,256]{1,0:T(8,128)(2,1)} %constant.35.place_band_ref) | copy-start | bytes 196612

commit v6 on v5

--- a/solution.py
+++ b/solution.py
@@ -26,8 +26,9 @@
 NDOSE = 4
 TAP_ROWS = 112
 GRID = 384
-EDGE = 32
+EDGE = 24
 TEDGE = 16
+SENT = 32
 GRAD_ROWS = 48
 BAND_ROWS = 32
 
@@ -197,16 +198,16 @@
     return jnp.concatenate([value[:, :LANES], value[:, LANES:]], axis=0).astype(BF)
 
 
-def picked(count, length, first):
+def picked(count, length, first, sent, held):
     row = lax.broadcasted_iota(jnp.int32, (count, length), 0) + first
-    row = jnp.where(row >= length, row - length, row)
+    row = jnp.where(row < 0, row + sent, jnp.where(row >= ROWS, row - ROWS, row + held))
     column = lax.broadcasted_iota(jnp.int32, (count, length), 1)
     return jnp.where(row == column, 1.0, 0.0).astype(BF)
 
 
 def edge_kernel(mask_ref, target_ref, dose_ref, out_ref, dose_rows_ref, mask_rows, target_rows, doses, sems):
     down = here(range(len(WINDOW))) < len(WINDOW) // 2
-    mask_from = pl.multiple_of(jnp.where(down, ROWS - EDGE, 0), EDGE)
+    mask_from = pl.multiple_of(jnp.where(down, ROWS - EDGE, 0), 8)
     target_from = pl.multiple_of(jnp.where(down, ROWS - TEDGE, 0), TEDGE)
     copies = [
         pltpu.make_async_copy(mask_ref.at[pl.ds(mask_from, EDGE)], mask_rows, sems.at[0]),
@@ -217,8 +218,11 @@
         copy.start()
     for copy in copies:
         copy.wait()
-    out_ref[:EDGE] = jnp.tanh(mask_rows[...]).astype(BF)
-    out_ref[EDGE:] = target_rows[...].astype(F32).astype(BF)
+    wanted = target_rows[...].astype(F32)
+    under = SENT - EDGE
+    beside = [wanted[under:, first : first + LANES] for first in range(0, W, LANES)]
+    rows = jnp.concatenate([jnp.tanh(mask_rows[...]), wanted[:under]], axis=0)
+    out_ref[...] = jnp.concatenate([rows, jnp.concatenate(beside, axis=0)], axis=1).astype(BF)
     for d in range(NDOSE):
         dose_rows_ref[d : d + 1] = jnp.full((1, ROWS), doses[d])
 
@@ -292,16 +296,20 @@
         start = here(STARTS)
         rows = spectra_ref[...]
         wanted = target_ref[...].astype(F32).astype(BF)
-        first, first_wanted = start - RIM, start
+        edges = (0, 0, 0, 0)
         if plan is OUTER:
-            rows = jnp.concatenate([dot(edge_ref[:EDGE], entry_ref[:W]).astype(BF), rows], axis=0)
-            wanted = jnp.concatenate([edge_ref[EDGE:], wanted], axis=0)
-            first, first_wanted = first + EDGE, first_wanted + TEDGE
-        pick = picked(u, rows.shape[0], first)
+            rows = jnp.concatenate([dot(edge_ref[:, :W], entry_ref[:W]).astype(BF), rows], axis=0)
+            under = SENT - EDGE
+            beside = edge_ref[:, W:].astype(F32)
+            beside = [beside[first : first + under] for first in range(0, SENT, under)]
+            sent = [edge_ref[:, :W].astype(F32)[EDGE:], jnp.concatenate(beside, axis=1)]
+            wanted = jnp.concatenate([jnp.concatenate(sent, axis=0).astype(BF), wanted], axis=0)
+            edges = (EDGE, SENT, TEDGE, TEDGE)
+        pick = picked(u, rows.shape[0], start - RIM, *edges[:2])
         mask_hat = dot(rows_ref[window_rows], stacked(dot(pick, rows))) * scale
         mask_re = mask_hat[:u]
         mask_im = mask_hat[u:]
-        band_ref[:count] = dot(picked(count, wanted.shape[0], first_wanted), wanted)
+        band_ref[:count] = dot(picked(count, wanted.shape[0], start, *edges[2:]), wanted)
         for group in range(NFOC * NK // 4):
             stacks = []
             for pair in range(2):
@@ -449,7 +457,7 @@
         edge_kernel,
         name="edge",
         out_shape=(
-            jax.ShapeDtypeStruct((EDGE + TEDGE, W), BF),
+            jax.ShapeDtypeStruct((SENT, W + LANES), BF),
             jax.ShapeDtypeStruct((NDOSE, ROWS), F32),
         ),
         in_specs=[pl.BlockSpec(memory_space=pl.ANY)] * 3,

time: 29.8 us -> 29.7 us (level)
  no operation moved by 1% of the time
where the time goes in v6:
time: 29.7 us; the launch traced here: 29.5 us
  blocking collectives  12.6 us (42%)
  Pallas kernels  8.13 us (27%)
  waiting for transfers between devices  5.86 us (20%)
  starting transfers between devices  2.05 us (7%)
  between operations  0.82 us (3%)
    all_to_all x1, blocking collectives, per_device(): blocks = lax.all_to_all(blocks, 'corner', 0, 0, tiled=True)  12.6 us
    ppermute x1, waiting for transfers between devices, per_device(): edge = lax.ppermute(edge, ('tile', 'corner'), pairs)  5.86 us
    pallas_call x1, Pallas kernels, per_device(): pl.pallas_call(image_kernel, name='image', out_shape=jax.ShapeDtypeStruct...  4.78 us
    ppermute x1, starting transfers between devices, per_device(): edge = lax.ppermute(edge, ('tile', 'corner'), pairs)  2.05 us
    pallas_call x1, Pallas kernels, per_device(): pl.pallas_call(prepare_kernel, name='prepare', out_shape=(jax.ShapeDtypeS...  1.4 us
    pallas_call x1, Pallas kernels, per_device(): pl.pallas_call(edge_kernel, name='edge', out_shape=(jax.ShapeDtypeStruct(...  1.12 us
    pallas_call x1, Pallas kernels, per_device(): pl.pallas_call(finish_kernel, name='finish', out_shape=(jax.ShapeDtypeStr...  0.83 us
  transfers between devices with their start and end apart: 1, of which 1 were waited for; matrix products, arithmetic and copies ran while one was open for 0% of the time, Pallas kernels for 5%

profile of v6, /device:TPU:2, one launch (start us, length us, event | category | flops | bytes accessed | tf_op | source)
XLA Modules:
  0.0 29.5 jit_solution(2678026756645010604)
XLA Ops:
  0.6 0.0 copy-start.5
  0.6 0.0 copy-start.3
  0.7 0.0 copy-start.2
  0.7 0.0 copy-start.10
  0.7 0.0 copy-start.11
  0.7 1.1 %edge.1 = (bf16[32,1280]{1,0:T(8,128)(2,1)S(1)}, f32[4,128]{1,0:T(4,128)S(1)}) custom-call(f32[128,1024]{1,0:T(8,128)} %mask_ref.3, s32[128,1024]{1,0:T(8,128)} %target_ref.3, f32[4]{0:T(128)} %dose_ref.1), custom_call_target="tpu_custom_call" | custom-call | flops 2000000000 | tf_op jit(solution)/shard_map/edge/pallas_call | solution.py:456
  1.8 2.1 %collective-permute-start = (bf16[32,1280]{1,0:T(8,128)(2,1)S(1)}, bf16[32,1280]{1,0:T(8,128)(2,1)S(1)}, u32[]{:S(2)}, u32[]{:S(2)}) collective-permute-start(bf16[32,1280]{1,0:T(8,128)(2,1)S(1)} %get-tuple-element.8), channel_id=1, source_target_pairs={{0,8},{1,9},{10,2},{12,4},{8,16},{9,17},{18,10},{20,12},{16,24},{1... | collective-permute-start | bytes 245768 | tf_op jit(solution)/shard_map/ppermute | solution.py:482
  3.9 0.0 copy-done.5
  3.9 0.0 copy-done.3
  3.9 0.0 copy-done.2
  3.9 0.0 copy-start.4
  3.9 0.0 copy-start.6
  3.9 0.0 copy-start.7
  3.9 0.0 copy-start.8
  4.0 0.0 copy-start.9
  4.0 1.4 %prepare.1 = (f32[48,96,256]{2,1,0:T(8,128)S(1)}, bf16[128,512]{1,0:T(8,128)(2,1)S(1)}, f32[128,128]{1,0:T(8,128)S(1)}) custom-call(f32[12,25,4,384]{3,2,1,0:T(4,128)S(1)} %bitcast.1, f32[128,1024]{1,0:T(8,128)S(1)} %copy-done.3, bf16[1376,512]{1,0:T(8,128)(2,1)S(1)} %copy-done.5), custom_call_target="tpu_custom_call" | custom-call | flops 1200000000 | tf_op jit(solution)/shard_map/prepare/pallas_call | solution.py:487
  5.4 5.9 %collective-permute-done.edge_ref = bf16[32,1280]{1,0:T(8,128)(2,1)S(1)} collective-permute-done((bf16[32,1280]{1,0:T(8,128)(2,1)S(1)}, bf16[32,1280]{1,0:T(8,128)(2,1)S(1)}, u32[]{:S(2)}, u32[]{:S(2)}) %collective-permute-start) | collective-permute-done | bytes 81952 | tf_op jit(solution)/shard_map/ppermute | solution.py:482
  11.2 0.0 copy-done.10
  11.2 0.0 copy-done.11
  11.2 0.0 copy-done.4
  11.2 0.0 copy-done.6
  11.3 0.0 copy-done.7
  11.3 0.0 copy-done.8
  11.3 0.0 copy-done.9
  11.3 0.0 copy-start
  11.3 0.0 copy-start.1
  11.3 4.8 %image.1 = bf16[8,80,128]{2,1,0:T(8,128)(2,1)S(1)} custom-call(f32[4,128]{1,0:T(4,128)S(1)} %get-tuple-element.7.dose_ref, bf16[32,1280]{1,0:T(8,128)(2,1)S(1)} %collective-permute-done.edge_ref, bf16[128,512]{1,0:T(8,128)(2,1)S(1)} %get-tuple-element.9.spectra_ref, s32[128,1024]{1,0:T(8,128)S(1)} %copy-done.4, ...), custom_call_target="tpu_custom_call" | custom-call | flops 4000000000 | bytes 8000000 | tf_op jit(solution)/shard_map/image/pallas_call | solution.py:505
  16.1 12.6 %all_to_all.5.blocks_ref = bf16[8,80,128]{2,1,0:T(8,128)(2,1)S(1)} all-to-all(bf16[8,80,128]{2,1,0:T(8,128)(2,1)S(1)} %image.1), channel_id=1, replica_groups=mesh['tile'=32,'corner'=8] {'corner'}, dimensions={0} | all-to-all | bytes 327680 | tf_op jit(solution)/shard_map/all_to_all | solution.py:535
  28.7 0.0 copy-done
  28.7 0.0 copy-done.1
  28.7 0.8 %finish.1 = (f32[128,128]{1,0:T(8,128)}, f32[128,128]{1,0:T(8,128)}) custom-call(bf16[8,80,128]{2,1,0:T(8,128)(2,1)S(1)} %all_to_all.5.blocks_ref, f32[128,128]{1,0:T(8,128)S(1)} %get-tuple-element.11.slope_ref, bf16[128,384]{1,0:T(8,128)(2,1)S(1)} %copy-done, bf16[128,256]{1,0:T(8,128)(2,1)S(1)} %copy-done.1), custom_call_target="tpu_custom_call" | custom-call | tf_op jit(solution)/shard_map/finish/pallas_call | solution.py:536
Async XLA Ops:
  0.6 3.2 %copy-start.5 = (bf16[1376,512]{1,0:T(8,128)(2,1)S(1)}, bf16[1376,512]{1,0:T(8,128)(2,1)}, u32[]{:S(2)}) copy-start(bf16[1376,512]{1,0:T(8,128)(2,1)} %constant.27.entry_ref) | copy-start | bytes 4227076
  0.6 3.2 %copy-start.3 = (f32[128,1024]{1,0:T(8,128)S(1)}, f32[128,1024]{1,0:T(8,128)}, u32[]{:S(2)}) copy-start(f32[128,1024]{1,0:T(8,128)} %mask_ref.3) | copy-start | bytes 1572868
  0.7 3.2 %copy-start.2 = (f32[4,12,25,384]{3,0,2,1:T(4,128)S(1)}, f32[4,12,25,384]{3,0,2,1:T(4,128)}, u32[]{:S(2)}) copy-start(f32[4,12,25,384]{3,0,2,1:T(4,128)} %param.15) | copy-start | bytes 5529604
  0.7 10.6 %copy-start.10 = (bf16[512,256]{1,0:T(8,128)(2,1)S(1)}, bf16[512,256]{1,0:T(8,128)(2,1)}, u32[]{:S(2)}) copy-start(bf16[512,256]{1,0:T(8,128)(2,1)} %constant.31.inverse_t_ref) | copy-start | bytes 786436
  0.7 10.6 %copy-start.11 = (bf16[256,512]{1,0:T(8,128)(2,1)S(1)}, bf16[256,512]{1,0:T(8,128)(2,1)}, u32[]{:S(2)}) copy-start(bf16[256,512]{1,0:T(8,128)(2,1)} %constant.28.inverse_ref) | copy-start | bytes 786436
  1.8 9.4 %collective-permute-start = (bf16[32,1280]{1,0:T(8,128)(2,1)S(1)}, bf16[32,1280]{1,0:T(8,128)(2,1)S(1)}, u32[]{:S(2)}, u32[]{:S(2)}) collective-permute-start(bf16[32,1280]{1,0:T(8,128)(2,1)S(1)} %get-tuple-element.8), channel_id=1, source_target_pairs={{0,8},{1,9},{10,2},{12,4},{8,16},{9,17},{18,10},{20,12},{16,24},{1... | collective-permute-start | bytes 245768 | tf_op jit(solution)/shard_map/ppermute | solution.py:482
  3.9 7.3 %copy-start.4 = (s32[128,1024]{1,0:T(8,128)S(1)}, s32[128,1024]{1,0:T(8,128)}, u32[]{:S(2)}) copy-start(s32[128,1024]{1,0:T(8,128)} %target_ref.3) | copy-start | bytes 1572868
  3.9 7.3 %copy-start.6 = (bf16[1024,512]{1,0:T(8,128)(2,1)S(1)}, bf16[1024,512]{1,0:T(8,128)(2,1)}, u32[]{:S(2)}) copy-start(bf16[1024,512]{1,0:T(8,128)(2,1)} %constant.32.interp_t_ref) | copy-start | bytes 3145732
  3.9 7.3 %copy-start.7 = (bf16[512,1024]{1,0:T(8,128)(2,1)S(1)}, bf16[512,1024]{1,0:T(8,128)(2,1)}, u32[]{:S(2)}) copy-start(bf16[512,1024]{1,0:T(8,128)(2,1)} %constant.30.forward_t_ref) | copy-start | bytes 3145732
  3.9 7.3 %copy-start.8 = (bf16[512,1024]{1,0:T(8,128)(2,1)S(1)}, bf16[512,1024]{1,0:T(8,128)(2,1)}, u32[]{:S(2)}) copy-start(bf16[512,1024]{1,0:T(8,128)(2,1)} %constant.29.interp_ref) | copy-start | bytes 3145732
  4.0 7.3 %copy-start.9 = (bf16[1136,256]{1,0:T(8,128)(2,1)S(1)}, bf16[1136,256]{1,0:T(8,128)(2,1)}, u32[]{:S(2)}) copy-start(bf16[1136,256]{1,0:T(8,128)(2,1)} %constant.33.rows_ref) | copy-start | bytes 1744900
  11.3 17.4 %copy-start = (bf16[128,384]{1,0:T(8,128)(2,1)S(1)}, bf16[128,384]{1,0:T(8,128)(2,1)}, u32[]{:S(2)}) copy-start(bf16[128,384]{1,0:T(8,128)(2,1)} %constant.34.place_grad_ref) | copy-start | bytes 294916
  11.3 17.4 %copy-start.1 = (bf16[128,256]{1,0:T(8,128)(2,1)S(1)}, bf16[128,256]{1,0:T(8,128)(2,1)}, u32[]{:S(2)}) copy-start(bf16[128,256]{1,0:T(8,128)(2,1)} %constant.35.place_band_ref) | copy-start | bytes 196612

commit v7 on v6

--- a/solution.py
+++ b/solution.py
@@ -45,7 +45,7 @@
 INNER = Plan(24, 24, 48, 1.62425)
 PLANS = (OUTER, OUTER, INNER, INNER, INNER, INNER, OUTER, OUTER)
 STARTS = tuple(sum(plan.share for plan in PLANS[:n]) - RIM for n in range(len(PLANS)))
-WINDOW = (0, 1, 7, 2, 6, 3, 4, 5)
+WINDOW = (0, 6, 7, 2, 1, 3, 4, 5)
 
 
 def low(table):

time: 29.7 us -> 29.7 us (level)
  no operation moved by 1% of the time
where the time goes in v7:
time: 29.7 us; the launch traced here: 29.5 us
  blocking collectives  12.6 us (42%)
  Pallas kernels  8.13 us (27%)
  waiting for transfers between devices  5.86 us (20%)
  starting transfers between devices  2.05 us (7%)
  between operations  0.82 us (3%)
    all_to_all x1, blocking collectives, per_device(): blocks = lax.all_to_all(blocks, 'corner', 0, 0, tiled=True)  12.6 us
    ppermute x1, waiting for transfers between devices, per_device(): edge = lax.ppermute(edge, ('tile', 'corner'), pairs)  5.86 us
    pallas_call x1, Pallas kernels, per_device(): pl.pallas_call(image_kernel, name='image', out_shape=jax.ShapeDtypeStruct...  4.78 us
    ppermute x1, starting transfers between devices, per_device(): edge = lax.ppermute(edge, ('tile', 'corner'), pairs)  2.05 us
    pallas_call x1, Pallas kernels, per_device(): pl.pallas_call(prepare_kernel, name='prepare', out_shape=(jax.ShapeDtypeS...  1.4 us
    pallas_call x1, Pallas kernels, per_device(): pl.pallas_call(edge_kernel, name='edge', out_shape=(jax.ShapeDtypeStruct(...  1.12 us
    pallas_call x1, Pallas kernels, per_device(): pl.pallas_call(finish_kernel, name='finish', out_shape=(jax.ShapeDtypeStr...  0.84 us
  transfers between devices with their start and end apart: 1, of which 1 were waited for; matrix products, arithmetic and copies ran while one was open for 0% of the time, Pallas kernels for 5%

profile of v7, /device:TPU:2, one launch (start us, length us, event | category | flops | bytes accessed | tf_op | source)
XLA Modules:
  0.0 29.5 jit_solution(5883109365979233523)
XLA Ops:
  0.6 0.0 copy-start.5
  0.6 0.0 copy-start.3
  0.7 0.0 copy-start.2
  0.7 0.0 copy-start.10
  0.7 0.0 copy-start.11
  0.7 1.1 %edge.1 = (bf16[32,1280]{1,0:T(8,128)(2,1)S(1)}, f32[4,128]{1,0:T(4,128)S(1)}) custom-call(f32[128,1024]{1,0:T(8,128)} %mask_ref.3, s32[128,1024]{1,0:T(8,128)} %target_ref.3, f32[4]{0:T(128)} %dose_ref.1), custom_call_target="tpu_custom_call" | custom-call | flops 2000000000 | tf_op jit(solution)/shard_map/edge/pallas_call | solution.py:456
  1.8 2.1 %collective-permute-start = (bf16[32,1280]{1,0:T(8,128)(2,1)S(1)}, bf16[32,1280]{1,0:T(8,128)(2,1)S(1)}, u32[]{:S(2)}, u32[]{:S(2)}) collective-permute-start(bf16[32,1280]{1,0:T(8,128)(2,1)S(1)} %get-tuple-element.8), channel_id=1, source_target_pairs={{0,8},{9,1},{10,2},{4,12},{8,16},{17,9},{18,10},{12,20},{16,24},{2... | collective-permute-start | bytes 245768 | tf_op jit(solution)/shard_map/ppermute | solution.py:482
  3.9 0.0 copy-done.5
  3.9 0.0 copy-done.3
  3.9 0.0 copy-done.2
  3.9 0.0 copy-start.4
  3.9 0.0 copy-start.6
  3.9 0.0 copy-start.7
  3.9 0.0 copy-start.8
  4.0 0.0 copy-start.9
  4.0 1.4 %prepare.1 = (f32[48,96,256]{2,1,0:T(8,128)S(1)}, bf16[128,512]{1,0:T(8,128)(2,1)S(1)}, f32[128,128]{1,0:T(8,128)S(1)}) custom-call(f32[12,25,4,384]{3,2,1,0:T(4,128)S(1)} %bitcast.1, f32[128,1024]{1,0:T(8,128)S(1)} %copy-done.3, bf16[1376,512]{1,0:T(8,128)(2,1)S(1)} %copy-done.5), custom_call_target="tpu_custom_call" | custom-call | flops 1200000000 | tf_op jit(solution)/shard_map/prepare/pallas_call | solution.py:487
  5.4 5.9 %collective-permute-done.edge_ref = bf16[32,1280]{1,0:T(8,128)(2,1)S(1)} collective-permute-done((bf16[32,1280]{1,0:T(8,128)(2,1)S(1)}, bf16[32,1280]{1,0:T(8,128)(2,1)S(1)}, u32[]{:S(2)}, u32[]{:S(2)}) %collective-permute-start) | collective-permute-done | bytes 81952 | tf_op jit(solution)/shard_map/ppermute | solution.py:482
  11.2 0.0 copy-done.10
  11.2 0.0 copy-done.11
  11.2 0.0 copy-done.4
  11.2 0.0 copy-done.6
  11.3 0.0 copy-done.7
  11.3 0.0 copy-done.8
  11.3 0.0 copy-done.9
  11.3 0.0 copy-start
  11.3 0.0 copy-start.1
  11.3 4.8 %image.1 = bf16[8,80,128]{2,1,0:T(8,128)(2,1)S(1)} custom-call(f32[4,128]{1,0:T(4,128)S(1)} %get-tuple-element.7.dose_ref, bf16[32,1280]{1,0:T(8,128)(2,1)S(1)} %collective-permute-done.edge_ref, bf16[128,512]{1,0:T(8,128)(2,1)S(1)} %get-tuple-element.9.spectra_ref, s32[128,1024]{1,0:T(8,128)S(1)} %copy-done.4, ...), custom_call_target="tpu_custom_call" | custom-call | flops 4000000000 | bytes 8000000 | tf_op jit(solution)/shard_map/image/pallas_call | solution.py:505
  16.1 12.6 %all_to_all.5.blocks_ref = bf16[8,80,128]{2,1,0:T(8,128)(2,1)S(1)} all-to-all(bf16[8,80,128]{2,1,0:T(8,128)(2,1)S(1)} %image.1), channel_id=1, replica_groups=mesh['tile'=32,'corner'=8] {'corner'}, dimensions={0} | all-to-all | bytes 327680 | tf_op jit(solution)/shard_map/all_to_all | solution.py:535
  28.7 0.0 copy-done
  28.7 0.0 copy-done.1
  28.7 0.8 %finish.1 = (f32[128,128]{1,0:T(8,128)}, f32[128,128]{1,0:T(8,128)}) custom-call(bf16[8,80,128]{2,1,0:T(8,128)(2,1)S(1)} %all_to_all.5.blocks_ref, f32[128,128]{1,0:T(8,128)S(1)} %get-tuple-element.11.slope_ref, bf16[128,384]{1,0:T(8,128)(2,1)S(1)} %copy-done, bf16[128,256]{1,0:T(8,128)(2,1)S(1)} %copy-done.1), custom_call_target="tpu_custom_call" | custom-call | tf_op jit(solution)/shard_map/finish/pallas_call | solution.py:536
Async XLA Ops:
  0.6 3.2 %copy-start.5 = (bf16[1376,512]{1,0:T(8,128)(2,1)S(1)}, bf16[1376,512]{1,0:T(8,128)(2,1)}, u32[]{:S(2)}) copy-start(bf16[1376,512]{1,0:T(8,128)(2,1)} %constant.27.entry_ref) | copy-start | bytes 4227076
  0.6 3.2 %copy-start.3 = (f32[128,1024]{1,0:T(8,128)S(1)}, f32[128,1024]{1,0:T(8,128)}, u32[]{:S(2)}) copy-start(f32[128,1024]{1,0:T(8,128)} %mask_ref.3) | copy-start | bytes 1572868
  0.7 3.2 %copy-start.2 = (f32[4,12,25,384]{3,0,2,1:T(4,128)S(1)}, f32[4,12,25,384]{3,0,2,1:T(4,128)}, u32[]{:S(2)}) copy-start(f32[4,12,25,384]{3,0,2,1:T(4,128)} %param.15) | copy-start | bytes 5529604
  0.7 10.6 %copy-start.10 = (bf16[512,256]{1,0:T(8,128)(2,1)S(1)}, bf16[512,256]{1,0:T(8,128)(2,1)}, u32[]{:S(2)}) copy-start(bf16[512,256]{1,0:T(8,128)(2,1)} %constant.31.inverse_t_ref) | copy-start | bytes 786436
  0.7 10.6 %copy-start.11 = (bf16[256,512]{1,0:T(8,128)(2,1)S(1)}, bf16[256,512]{1,0:T(8,128)(2,1)}, u32[]{:S(2)}) copy-start(bf16[256,512]{1,0:T(8,128)(2,1)} %constant.28.inverse_ref) | copy-start | bytes 786436
  1.8 9.4 %collective-permute-start = (bf16[32,1280]{1,0:T(8,128)(2,1)S(1)}, bf16[32,1280]{1,0:T(8,128)(2,1)S(1)}, u32[]{:S(2)}, u32[]{:S(2)}) collective-permute-start(bf16[32,1280]{1,0:T(8,128)(2,1)S(1)} %get-tuple-element.8), channel_id=1, source_target_pairs={{0,8},{9,1},{10,2},{4,12},{8,16},{17,9},{18,10},{12,20},{16,24},{2... | collective-permute-start | bytes 245768 | tf_op jit(solution)/shard_map/ppermute | solution.py:482
  3.9 7.3 %copy-start.4 = (s32[128,1024]{1,0:T(8,128)S(1)}, s32[128,1024]{1,0:T(8,128)}, u32[]{:S(2)}) copy-start(s32[128,1024]{1,0:T(8,128)} %target_ref.3) | copy-start | bytes 1572868
  3.9 7.3 %copy-start.6 = (bf16[1024,512]{1,0:T(8,128)(2,1)S(1)}, bf16[1024,512]{1,0:T(8,128)(2,1)}, u32[]{:S(2)}) copy-start(bf16[1024,512]{1,0:T(8,128)(2,1)} %constant.32.interp_t_ref) | copy-start | bytes 3145732
  3.9 7.3 %copy-start.7 = (bf16[512,1024]{1,0:T(8,128)(2,1)S(1)}, bf16[512,1024]{1,0:T(8,128)(2,1)}, u32[]{:S(2)}) copy-start(bf16[512,1024]{1,0:T(8,128)(2,1)} %constant.30.forward_t_ref) | copy-start | bytes 3145732
  3.9 7.3 %copy-start.8 = (bf16[512,1024]{1,0:T(8,128)(2,1)S(1)}, bf16[512,1024]{1,0:T(8,128)(2,1)}, u32[]{:S(2)}) copy-start(bf16[512,1024]{1,0:T(8,128)(2,1)} %constant.29.interp_ref) | copy-start | bytes 3145732
  4.0 7.3 %copy-start.9 = (bf16[1136,256]{1,0:T(8,128)(2,1)S(1)}, bf16[1136,256]{1,0:T(8,128)(2,1)}, u32[]{:S(2)}) copy-start(bf16[1136,256]{1,0:T(8,128)(2,1)} %constant.33.rows_ref) | copy-start | bytes 1744900
  11.3 17.4 %copy-start = (bf16[128,384]{1,0:T(8,128)(2,1)S(1)}, bf16[128,384]{1,0:T(8,128)(2,1)}, u32[]{:S(2)}) copy-start(bf16[128,384]{1,0:T(8,128)(2,1)} %constant.34.place_grad_ref) | copy-start | bytes 294916
  11.3 17.4 %copy-start.1 = (bf16[128,256]{1,0:T(8,128)(2,1)S(1)}, bf16[128,256]{1,0:T(8,128)(2,1)}, u32[]{:S(2)}) copy-start(bf16[128,256]{1,0:T(8,128)(2,1)} %constant.35.place_band_ref) | copy-start | bytes 196612
